TPU v7x, 32 devices: a whole 2x2x4 slice. The times are simulated.
32 devices in a mesh: dp: 8 (over z, y), mp: 4 (over x, core).
Axes of the slice: x: 2, y: 2, z: 4, core: 2. Of those that a mesh axis runs over, the one named last changes fastest.
Arguments:
- table: float32 [65536, 512], P('dp', 'mp'), may hold values from -6 to 6
- first_moment: float32 [65536, 512], P('dp', 'mp'), may hold values from -1.8 to 1.8
- second_moment: float32 [65536, 512], P('dp', 'mp'), may hold values from 0.01 to 1
- grads: bfloat16 [16384, 512], P('dp', 'mp'), may hold values from -108 to 108
- ids: int32 [16384], P('dp'), may hold values from 0 to 65535, as said below
Outputs:
- new_table: float32 [65536, 512], P('dp', 'mp')
- new_first: float32 [65536, 512], P('dp', 'mp')
- new_second: float32 [65536, 512], P('dp', 'mp')
Inputs may be any that keep to these rules, and one draw needn't show every extreme that they name: `ids`: the positions of one device name at most 1024 positions' worth of rows of any one owner (rows k * 8192 to (k + 1) * 8192 - 1) and at most 256 distinct rows of one owner; in every draw one owner reaches both bounds on every device.
All inputs are finite; a program needn't handle non-finite values.
Results may differ from a plain program's by a relative error of at most 0.0003.
Values may be sent and summed in bfloat16 or wider, within the bound.
No kernel may reach another device: no remote copies, remote signals or barrier semaphores. Data moves between devices by JAX's collectives and lax.ppermute only.
A program may use at most 64 MiB of HBM per device.

v0:
```python
import jax
import jax.numpy as jnp
from jax import lax
from jax.sharding import PartitionSpec as P

beta_first = 0.9
beta_second = 0.999
learn_rate = 0.01
decay_rate = 0.1
adam_eps = 1e-08
first_fix = 0.9999734386
second_fix = 0.0952078529


def block_size():
    return 512


def block_starts(count, step):
    return jnp.arange(0, count, step, dtype=jnp.int32)


def pack_slots(dest, local_row, values, slots, rows_dev):
    step = block_size()

    def pack_one_block(start):
        target = start + jnp.arange(step, dtype=jnp.int32)
        match = dest[None, :] == target[:, None]
        summed = jnp.dot(match.astype(jnp.bfloat16), values, preferred_element_type=jnp.float32)
        marks = jnp.min(jnp.where(match, local_row[None, :], rows_dev), axis=1)
        return (summed, marks)

    summed, marks = lax.map(pack_one_block, block_starts(slots, step))
    return (summed.reshape(slots, values.shape[1]), marks.reshape(slots))


def gather_rows(got_row, got, rows_dev):
    step = block_size()

    def gather_one_block(start):
        target = start + jnp.arange(step, dtype=jnp.int32)
        match = got_row[None, :] == target[:, None]
        return jnp.dot(
            match.astype(jnp.float32),
            got,
            precision=lax.Precision.HIGHEST,
            preferred_element_type=jnp.float32,
        )

    return lax.map(gather_one_block, block_starts(rows_dev, step)).reshape(rows_dev, got.shape[1])


def body(table, first_moment, second_moment, grads, ids):
    peers = lax.axis_size("dp")
    rows_dev = table.shape[0]
    width = table.shape[1]
    tok_dev = grads.shape[0]
    room = tok_dev // peers
    owner = ids // rows_dev
    local_row = ids - owner * rows_dev
    place = jnp.arange(tok_dev, dtype=jnp.int32)
    step = block_size()

    def first_block(start):
        here = start + jnp.arange(step, dtype=jnp.int32)
        mine = lax.dynamic_slice_in_dim(ids, start, step)
        earlier = jnp.logical_and(ids[None, :] == mine[:, None], place[None, :] < here[:, None])
        return jnp.logical_not(jnp.any(earlier, axis=1))

    leading = lax.map(first_block, block_starts(tok_dev, step)).reshape(tok_dev)

    def rank_block(start):
        mine = lax.dynamic_slice_in_dim(ids, start, step)
        mine_owner = lax.dynamic_slice_in_dim(owner, start, step)
        below = (
            leading[None, :]
            & (owner[None, :] == mine_owner[:, None])
            & (ids[None, :] < mine[:, None])
        )
        return jnp.sum(below.astype(jnp.int32), axis=1)

    rank = lax.map(rank_block, block_starts(tok_dev, step)).reshape(tok_dev)
    dest = owner * room + rank
    slots = peers * room
    sums, marker = pack_slots(dest, local_row, grads, slots, rows_dev)
    row_marks = marker.astype(jnp.float32).reshape(peers, room)
    got, got_rows = (
        lax.all_to_all(
            sums.reshape(peers, room, width), "dp", split_axis=0, concat_axis=0, tiled=True
        ),
        lax.all_to_all(row_marks, "dp", split_axis=0, concat_axis=0, tiled=True),
    )
    got_index = got_rows.reshape(slots).astype(jnp.int32)
    grad_rows = gather_rows(got_index, got.reshape(slots, width), rows_dev)
    local_sum = jnp.sum(grad_rows * grad_rows)
    total = lax.psum(local_sum, ("dp", "mp"))
    limit = jnp.sqrt(jnp.float32(tok_dev * peers * width * lax.axis_size("mp")))
    scale = limit / jnp.maximum(jnp.sqrt(total), limit)
    clipped = scale * grad_rows
    new_first = beta_first * first_moment + (1.0 - beta_first) * clipped
    new_second = beta_second * second_moment + (1.0 - beta_second) * clipped * clipped
    first_hat = new_first / first_fix
    second_hat = new_second / second_fix
    new_table = table - learn_rate * (
        first_hat / (jnp.sqrt(second_hat) + adam_eps) + decay_rate * table
    )
    return (new_table, new_first, new_second)


def solution(mesh):
    in_specs = (P("dp", "mp"), P("dp", "mp"), P("dp", "mp"), P("dp", "mp"), P("dp"))
    out_specs = (P("dp", "mp"), P("dp", "mp"), P("dp", "mp"))
    return jax.shard_map(body, mesh=mesh, in_specs=in_specs, out_specs=out_specs, check_vma=False)
```

profile of v0, /device:TPU:0, one launch (start us, length us, event | category | flops | bytes accessed | tf_op | source)
XLA Modules:
  0.0 222.1 jit_solution(6579937107355162544)
XLA Ops:
  1.4 22.3 %while.46 = (s32[]{:T(128)}, pred[4,512]{1,0:T(4,128)(4,1)S(1)}, s32[2048]{0:T(1024)}, s32[4]{0:T(128)S(1)}, s32[]{:T(128)}, /*index=5*/s32[]{:T(128)}, s32[]{:T(128)}) while((s32[]{:T(128)}, pred[4,512]{1,0:T(4,128)(4,1)S(1)}, s32[2048]{0:T(1024)}, s32[4]{0:T(128)S(1)}, s32[]{:T(128)}, /*index=5*/s32[]{:T(128)}, s32[]{:T(128)}) %tuple.67), condition=%wide.region_2.3_spmd.clone, body=%wide.region_0.2_spmd.clone.sunk | while | flops 4194821 | bytes 22159 | solution.py:70
  23.7 20.1 %while.43 = (s32[]{:T(128)}, s32[4,512]{1,0:T(4,128)S(1)}, pred[4,512]{1,0:T(4,128)(4,1)S(1)}, s32[2048]{0:T(1024)S(1)}, s32[4]{0:T(128)S(1)}, /*index=5*/s32[2048]{0:T(1024)}, s32[]{:T(128)}, s32[]{:T(128)}, s32[]{:T(128)}) while((s32[]{:T(128)}, s32[4,512]{1,0:T(4,128)S(1)}, pred[4,512]{1,0:T(4,128)(4,1)S(1)}, s32[2048]{0:T(1024)S(1)}, ...), condition=%wide.region_5.6_spmd, body=%wide.region_3.5_spmd.sunk | while | flops 6290949 | bytes 41119 | solution.py:82
  44.5 18.4 %while.44 = (s32[]{:T(128)}, f32[4,512,128]{2,1,0:T(8,128)}, s32[4,512]{1,0:T(4,128)S(1)}, s32[2048]{0:T(1024)S(1)}, s32[4]{0:T(128)S(1)}, /*index=5*/bf16[2048,...) while((s32[]{:T(128)}, f32[4,512,128]{2,1,0:T(8,128)}, s32[4,512]{1,0:T(4,128)S(1)}, ...), condition=%wide.region_8.9_spmd, body=%wide.region_6.8_spmd.sunk | while | flops 272629760 | bytes 823421 | solution.py:33
  63.0 13.6 %all_to_all.11 = f32[8,1,256]{2,1,0:T(1,128)S(1)} all-to-all(f32[8,1,256]{2,1,0:T(1,128)S(1)} %convert_element_type.26), channel_id=1, replica_groups=mesh['dp'=8,'mp'=4] {'dp'}, dimensions={0} | all-to-all | bytes 16384 | tf_op jit(solution)/shard_map/all_to_all | solution.py:91
  76.6 3.6 %all-to-all-start.1 = ((f32[8,256,128]{2,1,0:T(8,128)}), f32[8,256,128]{2,1,0:T(8,128)S(1)}, u32[]{:S(2)}, u32[]{:S(2)}) async-start(f32[8,256,128]{2,1,0:T(8,128)} %bitcast.8), calls=%async_computation.1 | async-start | bytes 2097152 | tf_op jit(solution)/shard_map/all_to_all | solution.py:88
  80.2 24.7 %all-to-all-done.1 = f32[8,256,128]{2,1,0:T(8,128)S(1)} async-done(((f32[8,256,128]{2,1,0:T(8,128)}), f32[8,256,128]{2,1,0:T(8,128)S(1)}, u32[]{:S(2)}, u32[]{:S(2)}) %all-to-all-start.1) | async-done | bytes 1048608 | tf_op jit(solution)/shard_map/all_to_all | solution.py:88
  104.9 62.8 %while.45 = (s32[]{:T(128)}, f32[16,512,128]{2,1,0:T(8,128)}, s32[2048]{0:T(1024)S(1)}, s32[16]{0:T(128)S(1)}, f32[2048,128]{1,0:T(8,128)S(1)}, /*index=5*/s32[]{:T(128)}) while((s32[]{:T(128)}, f32[16,512,128]{2,1,0:T(8,128)}, s32[2048]{0:T(1024)S(1)}, s32[16]{0:T(128)S(1)}, f32[2048,128]{1,0:T(8,128)S(1)}, /*index=5*/s32[]{:T(128)}) %tuple.81), condition=%wide.region_10.11_spmd, body=%wide.region_9.10_spmd.sunk | while | flops 1611661824 | bytes 1323105 | solution.py:50
  106.1 2.7 %fusion.47 = f32[16,512,128]{2,1,0:T(8,128)} fusion(f32[16,512,128]{2,1,0:T(8,128)} %get-tuple-element.409, s32[]{:T(128)S(6)} %copy.40, f32[2048,128]{1,0:T(8,128)S(1)} %get-tuple-element.418, s32[2048]{0:T(1024)S(1)} %get-tuple-element.416, s32[512]{0:T(512)S(1)} %iota_add_fusion.7), kind=kOutput, calls=%fused_computation.16.clone.1 | convolution fusion | flops 1611661312 | bytes 1320964 | tf_op jit(solution)/shard_map/while/body/eval_jaxpr/dot_general | solution.py:43
  113.9 2.7 %fusion.47 = f32[16,512,128]{2,1,0:T(8,128)} fusion(f32[16,512,128]{2,1,0:T(8,128)} %get-tuple-element.409, s32[]{:T(128)S(6)} %copy.40, f32[2048,128]{1,0:T(8,128)S(1)} %get-tuple-element.418, s32[2048]{0:T(1024)S(1)} %get-tuple-element.416, s32[512]{0:T(512)S(1)} %iota_add_fusion.7), kind=kOutput, calls=%fused_computation.16.clone.1 | convolution fusion | flops 1611661312 | bytes 1320964 | tf_op jit(solution)/shard_map/while/body/eval_jaxpr/dot_general | solution.py:43
  117.9 2.7 %fusion.47 = f32[16,512,128]{2,1,0:T(8,128)} fusion(f32[16,512,128]{2,1,0:T(8,128)} %get-tuple-element.409, s32[]{:T(128)S(6)} %copy.40, f32[2048,128]{1,0:T(8,128)S(1)} %get-tuple-element.418, s32[2048]{0:T(1024)S(1)} %get-tuple-element.416, s32[512]{0:T(512)S(1)} %iota_add_fusion.7), kind=kOutput, calls=%fused_computation.16.clone.1 | convolution fusion | flops 1611661312 | bytes 1320964 | tf_op jit(solution)/shard_map/while/body/eval_jaxpr/dot_general | solution.py:43
  121.8 2.7 %fusion.47 = f32[16,512,128]{2,1,0:T(8,128)} fusion(f32[16,512,128]{2,1,0:T(8,128)} %get-tuple-element.409, s32[]{:T(128)S(6)} %copy.40, f32[2048,128]{1,0:T(8,128)S(1)} %get-tuple-element.418, s32[2048]{0:T(1024)S(1)} %get-tuple-element.416, s32[512]{0:T(512)S(1)} %iota_add_fusion.7), kind=kOutput, calls=%fused_computation.16.clone.1 | convolution fusion | flops 1611661312 | bytes 1320964 | tf_op jit(solution)/shard_map/while/body/eval_jaxpr/dot_general | solution.py:43
  125.7 2.7 %fusion.47 = f32[16,512,128]{2,1,0:T(8,128)} fusion(f32[16,512,128]{2,1,0:T(8,128)} %get-tuple-element.409, s32[]{:T(128)S(6)} %copy.40, f32[2048,128]{1,0:T(8,128)S(1)} %get-tuple-element.418, s32[2048]{0:T(1024)S(1)} %get-tuple-element.416, s32[512]{0:T(512)S(1)} %iota_add_fusion.7), kind=kOutput, calls=%fused_computation.16.clone.1 | convolution fusion | flops 1611661312 | bytes 1320964 | tf_op jit(solution)/shard_map/while/body/eval_jaxpr/dot_general | solution.py:43
  129.6 2.7 %fusion.47 = f32[16,512,128]{2,1,0:T(8,128)} fusion(f32[16,512,128]{2,1,0:T(8,128)} %get-tuple-element.409, s32[]{:T(128)S(6)} %copy.40, f32[2048,128]{1,0:T(8,128)S(1)} %get-tuple-element.418, s32[2048]{0:T(1024)S(1)} %get-tuple-element.416, s32[512]{0:T(512)S(1)} %iota_add_fusion.7), kind=kOutput, calls=%fused_computation.16.clone.1 | convolution fusion | flops 1611661312 | bytes 1320964 | tf_op jit(solution)/shard_map/while/body/eval_jaxpr/dot_general | solution.py:43
  133.6 2.7 %fusion.47 = f32[16,512,128]{2,1,0:T(8,128)} fusion(f32[16,512,128]{2,1,0:T(8,128)} %get-tuple-element.409, s32[]{:T(128)S(6)} %copy.40, f32[2048,128]{1,0:T(8,128)S(1)} %get-tuple-element.418, s32[2048]{0:T(1024)S(1)} %get-tuple-element.416, s32[512]{0:T(512)S(1)} %iota_add_fusion.7), kind=kOutput, calls=%fused_computation.16.clone.1 | convolution fusion | flops 1611661312 | bytes 1320964 | tf_op jit(solution)/shard_map/while/body/eval_jaxpr/dot_general | solution.py:43
  145.3 2.7 %fusion.47 = f32[16,512,128]{2,1,0:T(8,128)} fusion(f32[16,512,128]{2,1,0:T(8,128)} %get-tuple-element.409, s32[]{:T(128)S(6)} %copy.40, f32[2048,128]{1,0:T(8,128)S(1)} %get-tuple-element.418, s32[2048]{0:T(1024)S(1)} %get-tuple-element.416, s32[512]{0:T(512)S(1)} %iota_add_fusion.7), kind=kOutput, calls=%fused_computation.16.clone.1 | convolution fusion | flops 1611661312 | bytes 1320964 | tf_op jit(solution)/shard_map/while/body/eval_jaxpr/dot_general | solution.py:43
  149.3 2.7 %fusion.47 = f32[16,512,128]{2,1,0:T(8,128)} fusion(f32[16,512,128]{2,1,0:T(8,128)} %get-tuple-element.409, s32[]{:T(128)S(6)} %copy.40, f32[2048,128]{1,0:T(8,128)S(1)} %get-tuple-element.418, s32[2048]{0:T(1024)S(1)} %get-tuple-element.416, s32[512]{0:T(512)S(1)} %iota_add_fusion.7), kind=kOutput, calls=%fused_computation.16.clone.1 | convolution fusion | flops 1611661312 | bytes 1320964 | tf_op jit(solution)/shard_map/while/body/eval_jaxpr/dot_general | solution.py:43
  153.2 2.7 %fusion.47 = f32[16,512,128]{2,1,0:T(8,128)} fusion(f32[16,512,128]{2,1,0:T(8,128)} %get-tuple-element.409, s32[]{:T(128)S(6)} %copy.40, f32[2048,128]{1,0:T(8,128)S(1)} %get-tuple-element.418, s32[2048]{0:T(1024)S(1)} %get-tuple-element.416, s32[512]{0:T(512)S(1)} %iota_add_fusion.7), kind=kOutput, calls=%fused_computation.16.clone.1 | convolution fusion | flops 1611661312 | bytes 1320964 | tf_op jit(solution)/shard_map/while/body/eval_jaxpr/dot_general | solution.py:43
  157.1 2.7 %fusion.47 = f32[16,512,128]{2,1,0:T(8,128)} fusion(f32[16,512,128]{2,1,0:T(8,128)} %get-tuple-element.409, s32[]{:T(128)S(6)} %copy.40, f32[2048,128]{1,0:T(8,128)S(1)} %get-tuple-element.418, s32[2048]{0:T(1024)S(1)} %get-tuple-element.416, s32[512]{0:T(512)S(1)} %iota_add_fusion.7), kind=kOutput, calls=%fused_computation.16.clone.1 | convolution fusion | flops 1611661312 | bytes 1320964 | tf_op jit(solution)/shard_map/while/body/eval_jaxpr/dot_general | solution.py:43
  161.0 2.7 %fusion.47 = f32[16,512,128]{2,1,0:T(8,128)} fusion(f32[16,512,128]{2,1,0:T(8,128)} %get-tuple-element.409, s32[]{:T(128)S(6)} %copy.40, f32[2048,128]{1,0:T(8,128)S(1)} %get-tuple-element.418, s32[2048]{0:T(1024)S(1)} %get-tuple-element.416, s32[512]{0:T(512)S(1)} %iota_add_fusion.7), kind=kOutput, calls=%fused_computation.16.clone.1 | convolution fusion | flops 1611661312 | bytes 1320964 | tf_op jit(solution)/shard_map/while/body/eval_jaxpr/dot_general | solution.py:43
  164.9 2.7 %fusion.47 = f32[16,512,128]{2,1,0:T(8,128)} fusion(f32[16,512,128]{2,1,0:T(8,128)} %get-tuple-element.409, s32[]{:T(128)S(6)} %copy.40, f32[2048,128]{1,0:T(8,128)S(1)} %get-tuple-element.418, s32[2048]{0:T(1024)S(1)} %get-tuple-element.416, s32[512]{0:T(512)S(1)} %iota_add_fusion.7), kind=kOutput, calls=%fused_computation.16.clone.1 | convolution fusion | flops 1611661312 | bytes 1320964 | tf_op jit(solution)/shard_map/while/body/eval_jaxpr/dot_general | solution.py:43
  167.6 3.9 %multiply_reduce_fusion = f32[]{:T(128)} fusion(f32[16,512,128]{2,1,0:T(8,128)} %get-tuple-element.131), kind=kLoop, calls=%fused_computation.27 | loop fusion | flops 2097151 | bytes 4194308 | tf_op jit(solution)/shard_map/reduce_sum | solution.py:95
  171.5 37.8 %psum.7 = f32[]{:T(128)} all-reduce(f32[]{:T(128)} %multiply_reduce_fusion), channel_id=1, replica_groups=mesh['dp'=8,'mp'=4] {'dp','mp'}, use_global_device_ids=true, to_apply=%region_12.13 | all-reduce | flops 1 | bytes 8 | tf_op jit(solution)/shard_map/psum | solution.py:96
  210.1 2.7 %broadcast_multiply_fusion = f32[16,512,128]{2,1,0:T(8,128)S(1)} fusion(f32[16,512,128]{2,1,0:T(8,128)} %get-tuple-element.131, f32[]{:T(128)S(6)} %div.34), kind=kLoop, calls=%fused_computation.28 | loop fusion | flops 1048576 | bytes 8388612 | tf_op jit(solution)/shard_map/mul | solution.py:99
  214.8 7.3 %multiply_subtract_fusion = (f32[8192,128]{1,0:T(8,128)}, f32[8192,128]{1,0:T(8,128)}, f32[8192,128]{1,0:T(8,128)}) fusion(f32[8192,128]{1,0:T(8,128)S(1)} %copy-done, f32[16,512,128]{2,1,0:T(8,128)S(1)} %broadcast_multiply_fusion, f32[8192,128]{1,0:T(8,128)S(1)} %copy-done.1, f32[8192,128]{1,0:T(8,128)} %param.15), kind=kLoop, calls=%fused_computation.26 | loop fusion | flops 15728640 | bytes 29360128 | tf_op jit(solution)/shard_map/sub | solution.py:104
  (124 shorter events, 78.3 us)
Async XLA Ops:
  76.6 28.3 %all-to-all-start.1 = ((f32[8,256,128]{2,1,0:T(8,128)}), f32[8,256,128]{2,1,0:T(8,128)S(1)}, u32[]{:S(2)}, u32[]{:S(2)}) async-start(f32[8,256,128]{2,1,0:T(8,128)} %bitcast.8), calls=%async_computation.1 | async-start | bytes 2097152 | tf_op jit(solution)/shard_map/all_to_all | solution.py:88
  210.1 3.5 %copy-start = (f32[8192,128]{1,0:T(8,128)S(1)}, f32[8192,128]{1,0:T(8,128)}, u32[]{:S(2)}) copy-start(f32[8192,128]{1,0:T(8,128)} %param.13) | copy-start | bytes 12582916
  210.1 4.7 %copy-start.1 = (f32[8192,128]{1,0:T(8,128)S(1)}, f32[8192,128]{1,0:T(8,128)}, u32[]{:S(2)}) copy-start(f32[8192,128]{1,0:T(8,128)} %param.14) | copy-start | bytes 12582916
where the time goes:
time: 224 us; the launch traced here: 222 us
  matrix products  53 us (24%)
  blocking collectives  51.4 us (23%)
  other arithmetic  48.4 us (22%)
  local copies, waits for them, and re-layouts  25.7 us (11%)
  waiting for transfers between devices  24.7 us (11%)
  loops' own time  13.8 us (6%)
  starting transfers between devices  3.56 us (2%)
    dot_general x16, matrix products, gather_one_block(): jnp.dot(match.astype(jnp.float32), got, precision=lax.Precision.HIGHEST,...  43 us
    psum x1, blocking collectives, body(): total = lax.psum(local_sum, ('dp', 'mp'))  37.8 us
    all_to_all x1, waiting for transfers between devices, body(): lax.all_to_all(sums.reshape(peers, room, width), 'dp', split_axis=0, conc...  24.7 us
    all_to_all x1, blocking collectives, body(): lax.all_to_all(row_marks, 'dp', split_axis=0, concat_axis=0, tiled=True)  13.6 us
    add x16, other arithmetic, gather_one_block(): target = start + jnp.arange(step, dtype=jnp.int32)  10.3 us
    dot_general x4, matrix products, pack_one_block(): jnp.dot(match.astype(jnp.bfloat16), values, preferred_element_type=jnp.fl...  10 us
    dynamic_slice x16, local copies, waits for them, and re-layouts, gather_rows(): lax.map(gather_one_block, block_starts(rows_dev, step))  9.31 us
    reduce_or x4, other arithmetic, first_block(): return jnp.logical_not(jnp.any(earlier, axis=1))  7.6 us
  transfers between devices with their start and end apart: 1, of which 1 were waited for; matrix products, arithmetic and copies ran while one was open for 0% of the time, Pallas kernels for 0%

commit v1 on v0

v1 whole, which is shorter than its diff:
```python
import functools
import math

import jax
import jax.numpy as jnp
from jax import lax
from jax.experimental import pallas as pl
from jax.experimental.pallas import tpu as pltpu
from jax.sharding import PartitionSpec as P

beta_first = 0.9
beta_second = 0.999
learn_rate = 0.01
decay_rate = 0.1
adam_eps = 1e-08
first_fix = 0.9999734386
second_fix = 0.0952078529

LANES = 128
META = 16
TOP = 32767.0
MIB = 2**20


def strip_rows(room):
    return -(-room // LANES)


def pack_kernel(peers, rows_dev, room, ids_ref, grads_ref, out_ref):
    tok = ids_ref.shape[1]
    per_owner = rows_dev // LANES
    buckets = peers * per_owner
    ids = ids_ref[...]
    high = ids // LANES
    low = ids - high * LANES
    f32, bf16 = jnp.float32, jnp.bfloat16

    def one_hot(keys, count):
        place = lax.broadcasted_iota(jnp.int32, (count, tok), 0)
        return jnp.where(place == keys, 1.0, 0.0).astype(bf16)

    high_hot = one_hot(high, buckets)
    low_hot = one_hot(low, LANES)
    counts = lax.dot_general(high_hot, low_hot, (((1,), (1,)), ((), ())), preferred_element_type=f32)
    present = jnp.where(counts > 0.0, 1.0, 0.0).astype(bf16)
    from_lane = lax.broadcasted_iota(jnp.int32, (LANES, LANES), 0)
    to_lane = lax.broadcasted_iota(jnp.int32, (LANES, LANES), 1)
    before = jnp.where(from_lane < to_lane, 1.0, 0.0).astype(bf16)
    within = jnp.dot(present, before, preferred_element_type=f32)
    totals = jnp.dot(present, jnp.ones((LANES, LANES), bf16), preferred_element_type=f32).astype(bf16)
    span = lax.broadcasted_iota(jnp.int32, (per_owner, per_owner), 0)
    other = lax.broadcasted_iota(jnp.int32, (per_owner, per_owner), 1)
    earlier = jnp.where(other < span, 1.0, 0.0).astype(bf16)
    offsets = [
        jnp.dot(earlier, totals[o * per_owner : (o + 1) * per_owner], preferred_element_type=f32)
        for o in range(peers)
    ]
    ranks = within + jnp.concatenate(offsets, axis=0)
    by_low = jnp.dot(ranks.T.astype(bf16), high_hot, preferred_element_type=f32)
    rank = jnp.sum(by_low * low_hot.astype(f32), axis=0, keepdims=True)
    rank = rank.astype(jnp.int32)

    sub = lax.broadcasted_iota(jnp.int32, (8, tok), 0)
    local_high = lax.rem(high, per_owner)
    digits = jnp.where(sub == 0, local_high, jnp.where(sub == 1, low, jnp.where(sub == 2, 1, 0)))
    digits = digits.astype(f32)
    aux = []
    for c in range(tok // LANES):
        tile = digits[:, c * LANES : (c + 1) * LANES]
        tile = jnp.concatenate([tile, jnp.zeros((LANES - 8, LANES), f32)], axis=0)
        aux.append(tile.T)
    wide = jnp.concatenate([grads_ref[...], jnp.concatenate(aux, axis=0).astype(bf16)], axis=1)

    lane = lax.broadcasted_iota(jnp.int32, (room, LANES), 1)
    meta = jnp.zeros((room, LANES), f32)
    for o in range(peers):
        inside = jnp.logical_and(ids >= o * rows_dev, ids < (o + 1) * rows_dev)
        match = one_hot(jnp.where(inside, rank, -1), room)
        summed = jnp.dot(match, wide, preferred_element_type=f32)
        sums = summed[:, :LANES]
        number = summed[:, LANES + 2 : LANES + 3]
        digit_high = summed[:, LANES : LANES + 1]
        digit_low = summed[:, LANES + 1 : LANES + 2]
        mark = jnp.where(
            number > 0.0,
            jnp.floor((digit_high * LANES + digit_low) / jnp.maximum(number, 1.0) + 0.5),
            float(rows_dev),
        )
        largest = jnp.max(jnp.abs(sums), axis=1, keepdims=True)
        power = jnp.ceil(jnp.log2(jnp.maximum(largest, 1e-30) * (1.0 / TOP)))
        code = jnp.clip(jnp.round(sums * jnp.exp2(-power)), -TOP, TOP)
        out_ref[o, :room, :] = code.astype(jnp.int32).astype(jnp.int16)
        meta = jnp.where(lane == 2 * o, mark, jnp.where(lane == 2 * o + 1, power, meta))
    strips = strip_rows(room)
    flat = meta.T.astype(jnp.int32)
    for o in range(peers):
        rows = []
        for k in range(2):
            for c in range(strips):
                piece = flat[2 * o + k : 2 * o + k + 1, c * LANES : min((c + 1) * LANES, room)]
                if piece.shape[1] < LANES:
                    piece = jnp.concatenate([piece, jnp.zeros((1, LANES - piece.shape[1]), jnp.int32)], axis=1)
                rows.append(piece)
        rows.append(jnp.zeros((META - len(rows), LANES), jnp.int32))
        out_ref[o, room:, :] = jnp.concatenate(rows, axis=0).astype(jnp.int16)


def add_kernel(peers, rows_dev, room, got_ref, acc_ref, part_ref, marks, values, slots, sem):
    strips = strip_rows(room)
    f32 = jnp.float32
    mark_rows, power_rows = [], []
    for s in range(peers):
        meta = got_ref[s, room:, :].astype(jnp.int32)
        mark_rows.append(meta[0:strips])
        power_rows.append(meta[strips : 2 * strips])
    marks[...] = jnp.concatenate(mark_rows, axis=0)
    copy = pltpu.make_async_copy(marks, slots, sem)
    copy.start()
    acc_ref[...] = jnp.zeros_like(acc_ref)
    powers = jnp.concatenate(power_rows, axis=0).astype(f32)
    count = powers.shape[0]
    padded = -(-count // LANES) * LANES
    if padded > count:
        powers = jnp.concatenate([powers, jnp.zeros((padded - count, LANES), f32)], axis=0)
    scales = jnp.exp2(powers).T
    for s in range(peers):
        for c in range(strips):
            high = min(LANES, room - c * LANES)
            code = got_ref[s, c * LANES : c * LANES + high, :].astype(jnp.int32).astype(f32)
            column = s * strips + c
            values[s * room + c * LANES : s * room + c * LANES + high, :] = code * scales[:high, column : column + 1]
    copy.wait()
    batch = 16
    per_strip = min(room, LANES) // batch

    def step(i, carry):
        strip = i // per_strip
        first = (i - strip * per_strip) * batch
        spots = [slots[strip, first + k] for k in range(batch)]
        base = pl.multiple_of(i * batch, batch)
        adds = [acc_ref[pl.ds(spots[k], 1), :] + values[pl.ds(base + k, 1), :] for k in range(batch)]
        for k in range(batch):
            acc_ref[pl.ds(spots[k], 1), :] = adds[k]
        return carry

    lax.fori_loop(0, peers * room // batch, step, 0)

    def square(i, total):
        block = acc_ref[pl.ds(pl.multiple_of(i * LANES, LANES), LANES), :]
        return total + jnp.sum((block * block).reshape(LANES // 8, 8, LANES), axis=0)

    total = lax.fori_loop(0, rows_dev // LANES, square, jnp.zeros((8, LANES), f32))
    total = jnp.sum(total, axis=0, keepdims=True)
    total = jnp.sum(total, axis=1, keepdims=True)
    part_ref[...] = jnp.broadcast_to(total[None], part_ref.shape)


def update_kernel(limit, parts_ref, grad_ref, table_ref, first_ref, second_ref, table_out, first_out, second_out, scale_ref):
    @pl.when(pl.program_id(0) == 0)
    def _():
        total = jnp.sum(parts_ref[...], axis=0)
        scale_ref[...] = limit / jnp.maximum(jnp.sqrt(total), limit)

    clipped = scale_ref[...] * grad_ref[...]
    new_first = beta_first * first_ref[...] + (1.0 - beta_first) * clipped
    new_second = beta_second * second_ref[...] + (1.0 - beta_second) * clipped * clipped
    first_hat = new_first / first_fix
    second_hat = new_second / second_fix
    table = table_ref[...]
    table_out[...] = table - learn_rate * (first_hat / (jnp.sqrt(second_hat) + adam_eps) + decay_rate * table)
    first_out[...] = new_first
    second_out[...] = new_second


def body(table, first_moment, second_moment, grads, ids):
    peers = lax.axis_size("dp")
    everyone = peers * lax.axis_size("mp")
    rows_dev, width = table.shape
    tok_dev = grads.shape[0]
    room = tok_dev // peers
    f32 = jnp.float32
    whole = pl.BlockSpec(memory_space=pltpu.VMEM)
    packed = pl.pallas_call(
        functools.partial(pack_kernel, peers, rows_dev, room),
        out_shape=jax.ShapeDtypeStruct((peers, room + META, width), jnp.int16),
        in_specs=[whole, whole],
        out_specs=whole,
        compiler_params=pltpu.CompilerParams(vmem_limit_bytes=40 * MIB),
        name="pack_rows",
    )(ids.reshape(1, tok_dev), grads)
    got = lax.all_to_all(packed, "dp", split_axis=0, concat_axis=0, tiled=True)
    strips = strip_rows(room)
    grad_rows, part = pl.pallas_call(
        functools.partial(add_kernel, peers, rows_dev, room),
        out_shape=(
            jax.ShapeDtypeStruct((rows_dev + 8, width), f32),
            jax.ShapeDtypeStruct((everyone, 1, width), f32),
        ),
        in_specs=[whole],
        out_specs=(whole, whole),
        scratch_shapes=[
            pltpu.VMEM((peers * strips, LANES), jnp.int32),
            pltpu.VMEM((peers * room, width), f32),
            pltpu.SMEM((peers * strips, LANES), jnp.int32),
            pltpu.SemaphoreType.DMA,
        ],
        compiler_params=pltpu.CompilerParams(vmem_limit_bytes=32 * MIB),
        name="add_rows",
    )(got)
    parts = lax.all_to_all(part, ("dp", "mp"), split_axis=0, concat_axis=0, tiled=True)
    limit = math.sqrt(tok_dev * everyone * width)
    step = 1024
    block = pl.BlockSpec((step, width), lambda i: (i, 0))
    return pl.pallas_call(
        functools.partial(update_kernel, limit),
        out_shape=tuple(jax.ShapeDtypeStruct((rows_dev, width), f32) for _ in range(3)),
        grid=(rows_dev // step,),
        in_specs=[pl.BlockSpec((everyone, 1, width), lambda i: (0, 0, 0)), block, block, block, block],
        out_specs=(block, block, block),
        scratch_shapes=[pltpu.VMEM((1, width), f32)],
        compiler_params=pltpu.CompilerParams(vmem_limit_bytes=24 * MIB),
        name="update_rows",
    )(parts, grad_rows, table, first_moment, second_moment)


def solution(mesh):
    in_specs = (P("dp", "mp"), P("dp", "mp"), P("dp", "mp"), P("dp", "mp"), P("dp"))
    out_specs = (P("dp", "mp"), P("dp", "mp"), P("dp", "mp"))
    return jax.shard_map(body, mesh=mesh, in_specs=in_specs, out_specs=out_specs, check_vma=False)
```

time: 224 us -> 66.1 us (0.30)
  matrix products: 53 us -> 0 us
  other arithmetic: 48.4 us -> 0 us
  waiting for transfers between devices: 24.7 us -> 0 us
  Pallas kernels: 0 us -> 23.9 us
  blocking collectives: 51.4 us -> 32.9 us
  local copies, waits for them, and re-layouts: 25.7 us -> 8.29 us
  loops' own time: 13.8 us -> 0 us
  starting transfers between devices: 3.56 us -> 0 us
    dot_general x20 -> x0, matrix products: 53 us -> none  [the longest x16 43 us: gather_one_block(): jnp.dot(match.astype(jnp.float32), got, precision=lax.Precision.HIGHEST,...]
    psum x1 -> x0, blocking collectives: 37.8 us -> none  [body(): total = lax.psum(local_sum, ('dp', 'mp'))]
    all_to_all x1 -> x0, waiting for transfers between devices: 24.7 us -> none  [body(): lax.all_to_all(sums.reshape(peers, room, width), 'dp', split_axis=0, conc...]
    pallas_call x0 -> x3, Pallas kernels: none -> 23.9 us  [the longest x1 9.41 us: body(): pl.pallas_call(functools.partial(add_kernel, peers, rows_dev, room), out_...]
    dynamic_slice x40 -> x0, local copies, waits for them, and re-layouts: 23.1 us -> none  [the longest x16 9.31 us: gather_rows(): lax.map(gather_one_block, block_starts(rows_dev, step))]
    all_to_all x1 -> x2, blocking collectives: 13.6 us -> 32.9 us  [the longest x1 23.1 us: body(): got = lax.all_to_all(packed, 'dp', split_axis=0, concat_axis=0, tiled=True)]
    add x24 -> x0, other arithmetic: 15.4 us -> none  [the longest x16 10.3 us: gather_one_block(): target = start + jnp.arange(step, dtype=jnp.int32)]
    another operation x4 -> x0, loops' own time: 13.8 us -> none  [the longest x1 6.83 us: body(): rank = lax.map(rank_block, block_starts(tok_dev, step)).reshape(tok_dev)]
  transfers between devices with their start and end apart: 1 -> 0, of which waited for: 1 -> 0; matrix products, arithmetic and copies ran while one was open for 0% -> 0% of each run, Pallas kernels for 0% -> 0%
where the time goes in v1:
time: 66.1 us; the launch traced here: 65.7 us
  blocking collectives  32.9 us (50%)
  Pallas kernels  23.9 us (36%)
  local copies, waits for them, and re-layouts  8.29 us (13%)
    all_to_all x1, blocking collectives, body(): got = lax.all_to_all(packed, 'dp', split_axis=0, concat_axis=0, tiled=True)  23.1 us
    all_to_all x1, blocking collectives, body(): lax.all_to_all(part, ('dp', 'mp'), split_axis=0, concat_axis=0, tiled=True)  9.8 us
    pallas_call x1, Pallas kernels, body(): pl.pallas_call(functools.partial(add_kernel, peers, rows_dev, room), out_...  9.41 us
    unnamed x10, local copies, waits for them, and re-layouts  8.29 us
    pallas_call x1, Pallas kernels, body(): pl.pallas_call(functools.partial(pack_kernel, peers, rows_dev, room), out...  7.65 us
    pallas_call x1, Pallas kernels, body(): pl.pallas_call(functools.partial(update_kernel, limit), out_shape=tuple((...  6.82 us

profile of v1, /device:TPU:0, one launch (start us, length us, event | category | flops | bytes accessed | tf_op | source)
XLA Modules:
  0.0 65.7 jit_solution(15991997617289029872)
XLA Ops:
  0.6 0.0 copy-start.3
  0.6 1.0 %copy-done.3 = bf16[2048,128]{1,0:T(8,128)(2,1)S(1)} copy-done((bf16[2048,128]{1,0:T(8,128)(2,1)S(1)}, bf16[2048,128]{1,0:T(8,128)(2,1)}, u32[]{:S(2)}) %copy-start.3) | copy-done | bytes 524312
  1.7 0.0 copy-start.4
  1.7 0.7 %copy-done.4 = s32[2048]{0:T(1024)S(1)} copy-done((s32[2048]{0:T(1024)S(1)}, s32[2048]{0:T(1024)}, u32[]{:S(2)}) %copy-start.4) | copy-done | bytes 8216
  2.4 7.7 %pack_rows.1 = s16[8,272,128]{2,1,0:T(8,128)(2,1)S(1)} custom-call(s32[1,2048]{1,0:T(1,128)S(1)} %bitcast.1, bf16[2048,128]{1,0:T(8,128)(2,1)S(1)} %copy-done.3), custom_call_target="tpu_custom_call" | custom-call | tf_op jit(solution)/shard_map/pack_rows/pallas_call | solution.py:183
  10.0 23.1 %all_to_all.10.got_ref = s16[8,272,128]{2,1,0:T(8,128)(2,1)S(1)} all-to-all(s16[8,272,128]{2,1,0:T(8,128)(2,1)S(1)} %pack_rows.1), channel_id=1, replica_groups=mesh['dp'=8,'mp'=4] {'dp'}, dimensions={0} | all-to-all | bytes 1114112 | tf_op jit(solution)/shard_map/all_to_all | solution.py:191
  33.1 9.4 %add_rows.1 = (f32[8200,128]{1,0:T(8,128)S(1)}, f32[32,1,128]{2,1,0:T(1,128)S(1)}) custom-call(s16[8,272,128]{2,1,0:T(8,128)(2,1)S(1)} %all_to_all.10.got_ref), custom_call_target="tpu_custom_call" | custom-call | tf_op jit(solution)/shard_map/add_rows/pallas_call | solution.py:193
  42.5 9.8 %all_to_all.11.parts_ref = f32[32,1,128]{2,1,0:T(1,128)S(1)} all-to-all(f32[32,1,128]{2,1,0:T(1,128)S(1)} %get-tuple-element.5), channel_id=1, replica_groups=mesh['dp'=8,'mp'=4] {'dp','mp'}, dimensions={0} | all-to-all | bytes 32768 | tf_op jit(solution)/shard_map/all_to_all | solution.py:210
  52.3 0.0 copy-start
  52.3 2.2 %copy-done = f32[8192,128]{1,0:T(8,128)S(1)} copy-done((f32[8192,128]{1,0:T(8,128)S(1)}, f32[8192,128]{1,0:T(8,128)}, u32[]{:S(2)}) %copy-start) | copy-done | bytes 4194328
  54.5 0.0 copy-start.1
  54.5 2.2 %copy-done.1 = f32[8192,128]{1,0:T(8,128)S(1)} copy-done((f32[8192,128]{1,0:T(8,128)S(1)}, f32[8192,128]{1,0:T(8,128)}, u32[]{:S(2)}) %copy-start.1) | copy-done | bytes 4194328
  56.7 0.0 copy-start.2
  56.7 2.2 %copy-done.2 = f32[8192,128]{1,0:T(8,128)S(1)} copy-done((f32[8192,128]{1,0:T(8,128)S(1)}, f32[8192,128]{1,0:T(8,128)}, u32[]{:S(2)}) %copy-start.2) | copy-done | bytes 4194328
  58.9 6.8 %update_rows.1 = (f32[8192,128]{1,0:T(8,128)}, f32[8192,128]{1,0:T(8,128)}, f32[8192,128]{1,0:T(8,128)}) custom-call(f32[32,1,128]{2,1,0:T(1,128)S(1)} %all_to_all.11.parts_ref, f32[8200,128]{1,0:T(8,128)S(1)} %get-tuple-element.6.grad_ref, f32[8192,128]{1,0:T(8,128)S(1)} %copy-done, f32[8192,128]{1,0:T(8,128)S(1)} %copy-done.1, f32[8192,128]{1,0:T(8,128)S(1)} %copy-done.2), custom_call_target="tpu_custom_call" | custom-call | tf_op jit(solution)/shard_map/update_rows/pallas_call | solution.py:214
Async XLA Ops:
  0.6 1.0 %copy-start.3 = (bf16[2048,128]{1,0:T(8,128)(2,1)S(1)}, bf16[2048,128]{1,0:T(8,128)(2,1)}, u32[]{:S(2)}) copy-start(bf16[2048,128]{1,0:T(8,128)(2,1)} %grads_ref.1) | copy-start | bytes 1572868
  1.7 0.7 %copy-start.4 = (s32[2048]{0:T(1024)S(1)}, s32[2048]{0:T(1024)}, u32[]{:S(2)}) copy-start(s32[2048]{0:T(1024)} %param.9) | copy-start | bytes 24580
  52.3 2.2 %copy-start = (f32[8192,128]{1,0:T(8,128)S(1)}, f32[8192,128]{1,0:T(8,128)}, u32[]{:S(2)}) copy-start(f32[8192,128]{1,0:T(8,128)} %table_ref.1) | copy-start | bytes 12582916
  54.5 2.2 %copy-start.1 = (f32[8192,128]{1,0:T(8,128)S(1)}, f32[8192,128]{1,0:T(8,128)}, u32[]{:S(2)}) copy-start(f32[8192,128]{1,0:T(8,128)} %first_ref.1) | copy-start | bytes 12582916
  56.7 2.2 %copy-start.2 = (f32[8192,128]{1,0:T(8,128)S(1)}, f32[8192,128]{1,0:T(8,128)}, u32[]{:S(2)}) copy-start(f32[8192,128]{1,0:T(8,128)} %second_ref.1) | copy-start | bytes 12582916

commit v2 on v1

v2 whole, which is shorter than its diff:
```python
import functools
import math

import jax
import jax.numpy as jnp
from jax import lax
from jax.experimental import pallas as pl
from jax.experimental.pallas import tpu as pltpu
from jax.sharding import PartitionSpec as P

beta_first = 0.9
beta_second = 0.999
learn_rate = 0.01
decay_rate = 0.1
adam_eps = 1e-08
first_fix = 0.9999734386
second_fix = 0.0952078529

LANES = 128
META = 16
TOP = 32767.0
MIB = 2**20


def strip_rows(room):
    return -(-room // LANES)


def partner(me, hop, peers):
    return me ^ hop if peers & (peers - 1) == 0 else lax.rem(me + hop, peers)


def pack_kernel(peers, rows_dev, room, ids_hbm, grads_hbm, table_hbm, first_hbm, second_hbm, *refs):
    outs, refs = refs[:peers], refs[peers:]
    table_ref, first_ref, second_ref, ids_ref, grads_ref, sems = refs
    pairs = (
        (ids_hbm, ids_ref),
        (grads_hbm, grads_ref),
        (table_hbm, table_ref),
        (first_hbm, first_ref),
        (second_hbm, second_ref),
    )
    copies = [pltpu.make_async_copy(a, b, sems.at[n]) for n, (a, b) in enumerate(pairs)]
    for copy in copies:
        copy.start()
    me = lax.axis_index("dp")
    copies[0].wait()
    tok = ids_ref.shape[1]
    per_owner = rows_dev // LANES
    buckets = peers * per_owner
    ids = ids_ref[...]
    high = ids // LANES
    low = ids - high * LANES
    f32, bf16 = jnp.float32, jnp.bfloat16

    def one_hot(keys, count):
        place = lax.broadcasted_iota(jnp.int32, (count, tok), 0)
        return jnp.where(place == keys, 1.0, 0.0).astype(bf16)

    high_hot = one_hot(high, buckets)
    low_hot = one_hot(low, LANES)
    counts = lax.dot_general(high_hot, low_hot, (((1,), (1,)), ((), ())), preferred_element_type=f32)
    present = jnp.where(counts > 0.0, 1.0, 0.0).astype(bf16)
    from_lane = lax.broadcasted_iota(jnp.int32, (LANES, LANES), 0)
    to_lane = lax.broadcasted_iota(jnp.int32, (LANES, LANES), 1)
    before = jnp.where(from_lane < to_lane, 1.0, 0.0).astype(bf16)
    within = jnp.dot(present, before, preferred_element_type=f32)
    totals = jnp.dot(present, jnp.ones((LANES, LANES), bf16), preferred_element_type=f32).astype(bf16)
    span = lax.broadcasted_iota(jnp.int32, (per_owner, per_owner), 0)
    other = lax.broadcasted_iota(jnp.int32, (per_owner, per_owner), 1)
    earlier = jnp.where(other < span, 1.0, 0.0).astype(bf16)
    offsets = [
        jnp.dot(earlier, totals[o * per_owner : (o + 1) * per_owner], preferred_element_type=f32)
        for o in range(peers)
    ]
    ranks = within + jnp.concatenate(offsets, axis=0)
    by_low = jnp.dot(ranks.T.astype(bf16), high_hot, preferred_element_type=f32)
    rank = jnp.sum(by_low * low_hot.astype(f32), axis=0, keepdims=True)
    rank = rank.astype(jnp.int32)

    sub = lax.broadcasted_iota(jnp.int32, (8, tok), 0)
    local_high = lax.rem(high, per_owner)
    digits = jnp.where(sub == 0, local_high, jnp.where(sub == 1, low, jnp.where(sub == 2, 1, 0)))
    digits = digits.astype(f32)
    aux = []
    for c in range(tok // LANES):
        tile = digits[:, c * LANES : (c + 1) * LANES]
        tile = jnp.concatenate([tile, jnp.zeros((LANES - 8, LANES), f32)], axis=0)
        aux.append(tile.T)
    copies[1].wait()
    wide = jnp.concatenate([grads_ref[...], jnp.concatenate(aux, axis=0).astype(bf16)], axis=1)

    lane = lax.broadcasted_iota(jnp.int32, (room, LANES), 1)
    meta = jnp.zeros((room, LANES), f32)
    for o in range(peers):
        low_id = partner(me, o, peers) * rows_dev
        inside = jnp.logical_and(ids >= low_id, ids < low_id + rows_dev)
        match = one_hot(jnp.where(inside, rank, -1), room)
        summed = jnp.dot(match, wide, preferred_element_type=f32)
        sums = summed[:, :LANES]
        number = summed[:, LANES + 2 : LANES + 3]
        digit_high = summed[:, LANES : LANES + 1]
        digit_low = summed[:, LANES + 1 : LANES + 2]
        mark = jnp.where(
            number > 0.0,
            jnp.floor((digit_high * LANES + digit_low) / jnp.maximum(number, 1.0) + 0.5),
            float(rows_dev),
        )
        largest = jnp.max(jnp.abs(sums), axis=1, keepdims=True)
        power = jnp.ceil(jnp.log2(jnp.maximum(largest, 1e-30) * (1.0 / TOP)))
        code = jnp.clip(jnp.round(sums * jnp.exp2(-power)), -TOP, TOP)
        outs[o][:room, :] = code.astype(jnp.int32).astype(jnp.int16)
        meta = jnp.where(lane == 2 * o, mark, jnp.where(lane == 2 * o + 1, power, meta))
    strips = strip_rows(room)
    flat = meta.T.astype(jnp.int32)
    for o in range(peers):
        rows = []
        for k in range(2):
            for c in range(strips):
                piece = flat[2 * o + k : 2 * o + k + 1, c * LANES : min((c + 1) * LANES, room)]
                if piece.shape[1] < LANES:
                    piece = jnp.concatenate([piece, jnp.zeros((1, LANES - piece.shape[1]), jnp.int32)], axis=1)
                rows.append(piece)
        rows.append(jnp.zeros((META - len(rows), LANES), jnp.int32))
        outs[o][room:, :] = jnp.concatenate(rows, axis=0).astype(jnp.int16)
    for copy in copies[2:]:
        copy.wait()


def join_kernel(peers, room, *refs):
    got, refs = refs[:peers], refs[peers:]
    grad_ref, part_ref, wide, sums_buf, marks_buf, slots, sem = refs
    strips = strip_rows(room)
    f32, bf16 = jnp.float32, jnp.bfloat16
    lines = peers * strips
    strip = min(room, LANES)
    mark_rows, power_rows = [], []
    for s in range(peers):
        meta = got[s][room:, :].astype(jnp.int32)
        mark_rows.append(meta[0:strips])
        power_rows.append(meta[strips : 2 * strips])
    marks = jnp.concatenate(mark_rows, axis=0)
    marks_buf[...] = marks
    copy = pltpu.make_async_copy(marks_buf, slots, sem)
    copy.start()
    grad_ref[...] = jnp.zeros_like(grad_ref)
    fill = jnp.zeros((LANES - 2 * lines, LANES), jnp.int32)
    both = jnp.concatenate([marks] + power_rows + [fill], axis=0).astype(f32)
    columns = both.T
    mark_columns = columns.astype(jnp.int32)
    scale_columns = jnp.exp2(columns)
    mark_line = jnp.concatenate([marks[k : k + 1, :strip] for k in range(lines)], axis=1)
    power_line = jnp.concatenate([both[lines + k : lines + k + 1, :strip] for k in range(lines)], axis=1)
    scale_line = jnp.exp2(power_line)
    for s in range(peers):
        code = got[s][:room, :].astype(jnp.int32)
        upper = (code + 128) >> 8
        lower = code - upper * 256
        halves = jnp.concatenate([upper.astype(f32), lower.astype(f32)], axis=1)
        wide[s * room : (s + 1) * room, :] = halves.astype(bf16)
    total = jnp.zeros((8, LANES), f32)
    per_block = max(1, min(256, peers * room) // strip)
    for first in range(0, lines, per_block):
        block = range(first, min(first + per_block, lines))
        same = [jnp.where(mark_columns[:strip, k : k + 1] == mark_line, scale_line, 0.0).astype(bf16) for k in block]
        sums = jnp.dot(jnp.concatenate(same, axis=0), wide[...], preferred_element_type=f32)
        sums = sums[:, :LANES] * 256.0 + sums[:, LANES:]
        sums_buf[first * strip : first * strip + len(block) * strip, :] = sums
        for n, k in enumerate(block):
            own = wide[k * strip : (k + 1) * strip, :].astype(f32)
            own = (own[:, :LANES] * 256.0 + own[:, LANES:]) * scale_columns[:strip, lines + k : lines + k + 1]
            product = own * sums[n * strip : (n + 1) * strip]
            total = total + jnp.sum(product.reshape(strip // 8, 8, LANES), axis=0)
        if first == 0:
            copy.wait()
        for k in block:
            for r in range(strip):
                grad_ref[pl.ds(slots[k, r], 1), :] = sums_buf[k * strip + r : k * strip + r + 1, :]
    total = jnp.sum(total, axis=0, keepdims=True)
    total = jnp.sum(total, axis=1, keepdims=True)
    part_ref[...] = jnp.broadcast_to(total[None], part_ref.shape)


def update_kernel(limit, step, parts_ref, grad_ref, table_ref, first_ref, second_ref, table_out, first_out, second_out,
                  table_buf, first_buf, second_buf, sems):
    total = jnp.sum(parts_ref[...], axis=0)
    scale = limit / jnp.maximum(jnp.sqrt(total), limit)
    rows = table_ref.shape[0]
    copies = []
    for n in range(rows // step):
        part = pl.ds(n * step, step)
        clipped = scale * grad_ref[part, :]
        new_first = beta_first * first_ref[part, :] + (1.0 - beta_first) * clipped
        first_buf[part, :] = new_first
        new_second = beta_second * second_ref[part, :] + (1.0 - beta_second) * clipped * clipped
        second_buf[part, :] = new_second
        change = (new_first * (learn_rate / first_fix)) / (jnp.sqrt(new_second * (1.0 / second_fix)) + adam_eps)
        table_buf[part, :] = table_ref[part, :] * (1.0 - learn_rate * decay_rate) - change
        for k, (a, b) in enumerate(((first_buf, first_out), (second_buf, second_out), (table_buf, table_out))):
            copy = pltpu.make_async_copy(a.at[part], b.at[part], sems.at[k, n])
            copy.start()
            copies.append(copy)
    for copy in copies:
        copy.wait()


def body(table, first_moment, second_moment, grads, ids):
    peers = lax.axis_size("dp")
    everyone = peers * lax.axis_size("mp")
    rows_dev, width = table.shape
    tok_dev = grads.shape[0]
    room = tok_dev // peers
    strips = strip_rows(room)
    f32 = jnp.float32
    shape = jax.ShapeDtypeStruct
    vmem = pl.BlockSpec(memory_space=pltpu.VMEM)
    hbm = pl.BlockSpec(memory_space=pltpu.HBM)
    in_hbm = lambda x: pltpu.with_memory_space_constraint(x, pltpu.HBM)
    in_vmem = lambda x: pltpu.with_memory_space_constraint(x, pltpu.VMEM)
    kept = pltpu.VMEM((rows_dev, width), f32)
    dense = shape((rows_dev, width), f32)
    *packed, table_kept, first_kept, second_kept = pl.pallas_call(
        functools.partial(pack_kernel, peers, rows_dev, room),
        out_shape=(shape((room + META, width), jnp.int16),) * peers + (kept,) * 3,
        in_specs=[hbm] * 5,
        out_specs=(vmem,) * (peers + 3),
        scratch_shapes=[
            pltpu.VMEM((1, tok_dev), jnp.int32),
            pltpu.VMEM((tok_dev, width), jnp.bfloat16),
            pltpu.SemaphoreType.DMA((5,)),
        ],
        compiler_params=pltpu.CompilerParams(vmem_limit_bytes=24 * MIB),
        name="pack_rows",
    )(*[in_hbm(x) for x in (ids.reshape(1, tok_dev), grads, table, first_moment, second_moment)])
    got = [packed[0]] + [None] * (peers - 1)
    for hop in range(peers - 1, 0, -1):
        pairs = [(i, int(partner(i, hop, peers)) if peers & (peers - 1) == 0 else (i + hop) % peers) for i in range(peers)]
        got[hop] = lax.ppermute(packed[hop], "dp", pairs)
    grad_rows, part = pl.pallas_call(
        functools.partial(join_kernel, peers, room),
        out_shape=(pltpu.VMEM((rows_dev + 8, width), f32), shape((everyone, 1, width), f32)),
        in_specs=[vmem] * peers,
        out_specs=(vmem,) * 2,
        scratch_shapes=[
            pltpu.VMEM((peers * room, 2 * width), jnp.bfloat16),
            pltpu.VMEM((peers * room, width), f32),
            pltpu.VMEM((peers * strips, LANES), jnp.int32),
            pltpu.SMEM((peers * strips, LANES), jnp.int32),
            pltpu.SemaphoreType.DMA,
        ],
        compiler_params=pltpu.CompilerParams(vmem_limit_bytes=16 * MIB),
        name="join_rows",
    )(got[0], *got[:0:-1])
    parts = lax.all_to_all(part, ("dp", "mp"), split_axis=0, concat_axis=0, tiled=True)
    limit = math.sqrt(tok_dev * everyone * width)
    step = math.gcd(1024, rows_dev)
    return pl.pallas_call(
        functools.partial(update_kernel, limit, step),
        out_shape=(dense,) * 3,
        in_specs=[vmem] * 5,
        out_specs=(hbm,) * 3,
        scratch_shapes=[pltpu.VMEM((rows_dev, width), f32)] * 3 + [pltpu.SemaphoreType.DMA((3, rows_dev // step))],
        compiler_params=pltpu.CompilerParams(vmem_limit_bytes=20 * MIB),
        name="update_rows",
    )(parts, *[in_vmem(x) for x in (grad_rows, table_kept, first_kept, second_kept)])


def solution(mesh):
    in_specs = (P("dp", "mp"), P("dp", "mp"), P("dp", "mp"), P("dp", "mp"), P("dp"))
    out_specs = (P("dp", "mp"), P("dp", "mp"), P("dp", "mp"))
    return jax.shard_map(body, mesh=mesh, in_specs=in_specs, out_specs=out_specs, check_vma=False)
```

time: 66.1 us -> 47.5 us (0.72)
  blocking collectives: 32.9 us -> 12.6 us
  starting transfers between devices: 0 us -> 13.3 us
  local copies, waits for them, and re-layouts: 8.29 us -> 0 us
  Pallas kernels: 23.9 us -> 15.9 us
  waiting for transfers between devices: 0 us -> 4.72 us
    all_to_all x1 -> x0, blocking collectives: 23.1 us -> none  [body(): got = lax.all_to_all(packed, 'dp', split_axis=0, concat_axis=0, tiled=True)]
    ppermute x0 -> x7, starting transfers between devices: none -> 13.3 us  [body(): got[hop] = lax.ppermute(packed[hop], 'dp', pairs)]
    unnamed x10 -> x0, local copies, waits for them, and re-layouts: 8.29 us -> none
    pallas_call x2, Pallas kernels: 16.2 us -> 9.2 us  [the longest x1 5.17 us: body(): pl.pallas_call(functools.partial(update_kernel, limit, step), out_shape=(...]
    ppermute x0 -> x7, waiting for transfers between devices: none -> 4.72 us  [body(): got[hop] = lax.ppermute(packed[hop], 'dp', pairs)]
    all_to_all x1, blocking collectives: 9.8 us -> 12.6 us  [body(): lax.all_to_all(part, ('dp', 'mp'), split_axis=0, concat_axis=0, tiled=True)]
    pallas_call x1, Pallas kernels: 7.65 us -> 6.67 us  [body(): pl.pallas_call(functools.partial(pack_kernel, peers, rows_dev, room), out...]
  transfers between devices with their start and end apart: 0 -> 7, of which waited for: 0 -> 3; matrix products, arithmetic and copies ran while one was open for 0% -> 0% of each run, Pallas kernels for 0% -> 0%
where the time goes in v2:
time: 47.5 us; the launch traced here: 47.3 us
  Pallas kernels  15.9 us (33%)
  starting transfers between devices  13.3 us (28%)
  blocking collectives  12.6 us (27%)
  waiting for transfers between devices  4.72 us (10%)
  between operations  0.82 us (2%)
    ppermute x7, starting transfers between devices, body(): got[hop] = lax.ppermute(packed[hop], 'dp', pairs)  13.3 us
    all_to_all x1, blocking collectives, body(): lax.all_to_all(part, ('dp', 'mp'), split_axis=0, concat_axis=0, tiled=True)  12.6 us
    pallas_call x1, Pallas kernels, body(): pl.pallas_call(functools.partial(pack_kernel, peers, rows_dev, room), out...  6.67 us
    pallas_call x1, Pallas kernels, body(): pl.pallas_call(functools.partial(update_kernel, limit, step), out_shape=(...  5.17 us
    ppermute x7, waiting for transfers between devices, body(): got[hop] = lax.ppermute(packed[hop], 'dp', pairs)  4.72 us
    pallas_call x1, Pallas kernels, body(): pl.pallas_call(functools.partial(join_kernel, peers, room), out_shape=(pl...  4.03 us
  transfers between devices with their start and end apart: 7, of which 3 were waited for; matrix products, arithmetic and copies ran while one was open for 0% of the time, Pallas kernels for 0%

profile of v2, /device:TPU:0, one launch (start us, length us, event | category | flops | bytes accessed | tf_op | source)
XLA Modules:
  0.0 47.3 jit_solution(6866998954884038607)
XLA Ops:
  0.6 6.7 %pack_rows.1 = (s16[272,128]{1,0:T(8,128)(2,1)S(1)}, s16[272,128]{1,0:T(8,128)(2,1)S(1)}, s16[272,128]{1,0:T(8,128)(2,1)S(1)}, s16[272,128]{1,0:T(8,128)(2,1)S(1...) custom-call(s32[1,2048]{1,0:T(1,128)} %bitcast.1, ...), custom_call_target="tpu_custom_call" | custom-call | tf_op jit(solution)/shard_map/pack_rows/pallas_call | solution.py:222
  7.3 6.1 %collective-permute-start = (s16[272,128]{1,0:T(8,128)(2,1)S(1)}, s16[272,128]{1,0:T(8,128)(2,1)S(1)}, u32[]{:S(2)}, u32[]{:S(2)}) collective-permute-start(s16[272,128]{1,0:T(8,128)(2,1)S(1)} %get-tuple-element.17), channel_id=1, source_target_pairs={{0,28},{4,24},{8,20},{12,16},{16,12},{20,8},{24,4},{28,0},{1,29},{... | collective-permute-start | bytes 208904 | tf_op jit(solution)/shard_map/ppermute | solution.py:238
  13.4 0.2 collective-permute-start.1
  13.6 0.7 %collective-permute-start.2 = (s16[272,128]{1,0:T(8,128)(2,1)S(1)}, s16[272,128]{1,0:T(8,128)(2,1)S(1)}, u32[]{:S(2)}, u32[]{:S(2)}) collective-permute-start(s16[272,128]{1,0:T(8,128)(2,1)S(1)} %get-tuple-element.19), channel_id=1, source_target_pairs={{0,20},{4,16},{8,28},{12,24},{16,4},{20,0},{24,12},{28,8},{1,21},{... | collective-permute-start | bytes 208904 | tf_op jit(solution)/shard_map/ppermute | solution.py:238
  14.3 2.0 %collective-permute-start.3 = (s16[272,128]{1,0:T(8,128)(2,1)S(1)}, s16[272,128]{1,0:T(8,128)(2,1)S(1)}, u32[]{:S(2)}, u32[]{:S(2)}) collective-permute-start(s16[272,128]{1,0:T(8,128)(2,1)S(1)} %get-tuple-element.20), channel_id=1, source_target_pairs={{0,16},{4,20},{8,24},{12,28},{16,0},{20,4},{24,8},{28,12},{1,17},{... | collective-permute-start | bytes 208904 | tf_op jit(solution)/shard_map/ppermute | solution.py:238
  16.4 2.3 %collective-permute-start.4 = (s16[272,128]{1,0:T(8,128)(2,1)S(1)}, s16[272,128]{1,0:T(8,128)(2,1)S(1)}, u32[]{:S(2)}, u32[]{:S(2)}) collective-permute-start(s16[272,128]{1,0:T(8,128)(2,1)S(1)} %get-tuple-element.21), channel_id=1, source_target_pairs={{0,12},{4,8},{8,4},{12,0},{16,28},{20,24},{24,20},{28,16},{1,13},{... | collective-permute-start | bytes 208904 | tf_op jit(solution)/shard_map/ppermute | solution.py:238
  18.7 0.0 collective-permute-done.refs_1_
  18.7 1.5 %collective-permute-start.5 = (s16[272,128]{1,0:T(8,128)(2,1)S(1)}, s16[272,128]{1,0:T(8,128)(2,1)S(1)}, u32[]{:S(2)}, u32[]{:S(2)}) collective-permute-start(s16[272,128]{1,0:T(8,128)(2,1)S(1)} %get-tuple-element.22), channel_id=1, source_target_pairs={{0,8},{4,12},{8,0},{12,4},{16,24},{20,28},{24,16},{28,20},{1,9},{5... | collective-permute-start | bytes 208904 | tf_op jit(solution)/shard_map/ppermute | solution.py:238
  20.1 0.0 collective-permute-done.1.refs_2_
  20.1 0.5 %collective-permute-start.6 = (s16[272,128]{1,0:T(8,128)(2,1)S(1)}, s16[272,128]{1,0:T(8,128)(2,1)S(1)}, u32[]{:S(2)}, u32[]{:S(2)}) collective-permute-start(s16[272,128]{1,0:T(8,128)(2,1)S(1)} %get-tuple-element.23), channel_id=1, source_target_pairs={{0,4},{4,0},{8,12},{12,8},{16,20},{20,16},{24,28},{28,24},{1,5},{5... | collective-permute-start | bytes 208904 | tf_op jit(solution)/shard_map/ppermute | solution.py:238
  20.6 3.6 %collective-permute-done.2.refs_3_ = s16[272,128]{1,0:T(8,128)(2,1)S(1)} collective-permute-done((s16[272,128]{1,0:T(8,128)(2,1)S(1)}, s16[272,128]{1,0:T(8,128)(2,1)S(1)}, u32[]{:S(2)}, u32[]{:S(2)}) %collective-permute-start.2) | collective-permute-done | bytes 69664 | tf_op jit(solution)/shard_map/ppermute | solution.py:238
  24.3 1.0 %collective-permute-done.3.refs_4_ = s16[272,128]{1,0:T(8,128)(2,1)S(1)} collective-permute-done((s16[272,128]{1,0:T(8,128)(2,1)S(1)}, s16[272,128]{1,0:T(8,128)(2,1)S(1)}, u32[]{:S(2)}, u32[]{:S(2)}) %collective-permute-start.3) | collective-permute-done | bytes 69664 | tf_op jit(solution)/shard_map/ppermute | solution.py:238
  25.3 0.0 collective-permute-done.4.refs_5_
  25.3 0.1 collective-permute-done.5.refs_6_
  25.3 0.0 collective-permute-done.6.refs_7_
  25.3 4.0 %join_rows.1 = (f32[8200,128]{1,0:T(8,128)S(1)}, f32[32,1,128]{2,1,0:T(1,128)S(1)}) custom-call(s16[272,128]{1,0:T(8,128)(2,1)S(1)} %get-tuple-element.16.refs_0_, s16[272,128]{1,0:T(8,128)(2,1)S(1)} %collective-permute-done.refs_1_, s16[272,128]{1,0:T(8,128)(2,1)S(1)} %collective-permute-done.1.refs_2_, s16[272,128]{1,0:T(8,128)(2,1)S(1)} %collective-permute-done.2.refs_3_, ...), custom_call_target="tpu_custom_call" | custom-call | tf_op jit(solution)/shard_map/join_rows/pallas_call | solution.py:239
  29.4 12.6 %all_to_all.5.parts_ref = f32[32,1,128]{2,1,0:T(1,128)S(1)} all-to-all(f32[32,1,128]{2,1,0:T(1,128)S(1)} %get-tuple-element.24), channel_id=1, replica_groups=mesh['dp'=8,'mp'=4] {'dp','mp'}, dimensions={0} | all-to-all | bytes 32768 | tf_op jit(solution)/shard_map/all_to_all | solution.py:254
  42.0 5.2 %update_rows.1 = (f32[8192,128]{1,0:T(8,128)}, f32[8192,128]{1,0:T(8,128)}, f32[8192,128]{1,0:T(8,128)}) custom-call(f32[32,1,128]{2,1,0:T(1,128)S(1)} %all_to_all.5.parts_ref, f32[8200,128]{1,0:T(8,128)S(1)} %get-tuple-element.25.grad_ref, f32[8192,128]{1,0:T(8,128)S(1)} %get-tuple-element.26.table_ref, f32[8192,128]{1,0:T(8,128)S(1)} %get-tuple-element.27.first_ref, ...), custom_call_target="tpu_custom_call" | custom-call | tf_op jit(solution)/shard_map/update_rows/pallas_call | solution.py:257
Async XLA Ops:
  7.3 11.4 %collective-permute-start = (s16[272,128]{1,0:T(8,128)(2,1)S(1)}, s16[272,128]{1,0:T(8,128)(2,1)S(1)}, u32[]{:S(2)}, u32[]{:S(2)}) collective-permute-start(s16[272,128]{1,0:T(8,128)(2,1)S(1)} %get-tuple-element.17), channel_id=1, source_target_pairs={{0,28},{4,24},{8,20},{12,16},{16,12},{20,8},{24,4},{28,0},{1,29},{... | collective-permute-start | bytes 208904 | tf_op jit(solution)/shard_map/ppermute | solution.py:238
  13.4 6.7 %collective-permute-start.1 = (s16[272,128]{1,0:T(8,128)(2,1)S(1)}, s16[272,128]{1,0:T(8,128)(2,1)S(1)}, u32[]{:S(2)}, u32[]{:S(2)}) collective-permute-start(s16[272,128]{1,0:T(8,128)(2,1)S(1)} %get-tuple-element.18), channel_id=1, source_target_pairs={{0,24},{4,28},{8,16},{12,20},{16,8},{20,12},{24,0},{28,4},{1,25},{... | collective-permute-start | bytes 208904 | tf_op jit(solution)/shard_map/ppermute | solution.py:238
  13.6 10.7 %collective-permute-start.2 = (s16[272,128]{1,0:T(8,128)(2,1)S(1)}, s16[272,128]{1,0:T(8,128)(2,1)S(1)}, u32[]{:S(2)}, u32[]{:S(2)}) collective-permute-start(s16[272,128]{1,0:T(8,128)(2,1)S(1)} %get-tuple-element.19), channel_id=1, source_target_pairs={{0,20},{4,16},{8,28},{12,24},{16,4},{20,0},{24,12},{28,8},{1,21},{... | collective-permute-start | bytes 208904 | tf_op jit(solution)/shard_map/ppermute | solution.py:238
  14.3 11.0 %collective-permute-start.3 = (s16[272,128]{1,0:T(8,128)(2,1)S(1)}, s16[272,128]{1,0:T(8,128)(2,1)S(1)}, u32[]{:S(2)}, u32[]{:S(2)}) collective-permute-start(s16[272,128]{1,0:T(8,128)(2,1)S(1)} %get-tuple-element.20), channel_id=1, source_target_pairs={{0,16},{4,20},{8,24},{12,28},{16,0},{20,4},{24,8},{28,12},{1,17},{... | collective-permute-start | bytes 208904 | tf_op jit(solution)/shard_map/ppermute | solution.py:238
  16.4 8.9 %collective-permute-start.4 = (s16[272,128]{1,0:T(8,128)(2,1)S(1)}, s16[272,128]{1,0:T(8,128)(2,1)S(1)}, u32[]{:S(2)}, u32[]{:S(2)}) collective-permute-start(s16[272,128]{1,0:T(8,128)(2,1)S(1)} %get-tuple-element.21), channel_id=1, source_target_pairs={{0,12},{4,8},{8,4},{12,0},{16,28},{20,24},{24,20},{28,16},{1,13},{... | collective-permute-start | bytes 208904 | tf_op jit(solution)/shard_map/ppermute | solution.py:238
  18.7 6.7 %collective-permute-start.5 = (s16[272,128]{1,0:T(8,128)(2,1)S(1)}, s16[272,128]{1,0:T(8,128)(2,1)S(1)}, u32[]{:S(2)}, u32[]{:S(2)}) collective-permute-start(s16[272,128]{1,0:T(8,128)(2,1)S(1)} %get-tuple-element.22), channel_id=1, source_target_pairs={{0,8},{4,12},{8,0},{12,4},{16,24},{20,28},{24,16},{28,20},{1,9},{5... | collective-permute-start | bytes 208904 | tf_op jit(solution)/shard_map/ppermute | solution.py:238
  20.1 5.2 %collective-permute-start.6 = (s16[272,128]{1,0:T(8,128)(2,1)S(1)}, s16[272,128]{1,0:T(8,128)(2,1)S(1)}, u32[]{:S(2)}, u32[]{:S(2)}) collective-permute-start(s16[272,128]{1,0:T(8,128)(2,1)S(1)} %get-tuple-element.23), channel_id=1, source_target_pairs={{0,4},{4,0},{8,12},{12,8},{16,20},{20,16},{24,28},{28,24},{1,5},{5... | collective-permute-start | bytes 208904 | tf_op jit(solution)/shard_map/ppermute | solution.py:238

commit v3 on v2

v3 whole, which is shorter than its diff:
```python
import functools
import math

import jax
import jax.numpy as jnp
from jax import lax
from jax.experimental import pallas as pl
from jax.experimental.pallas import tpu as pltpu
from jax.sharding import PartitionSpec as P

beta_first = 0.9
beta_second = 0.999
learn_rate = 0.01
decay_rate = 0.1
adam_eps = 1e-08
first_fix = 0.9999734386
second_fix = 0.0952078529

LANES = 128
META = 16
TOP = 32767.0
MIB = 2**20


def strip_rows(room):
    return -(-room // LANES)


def relative(me, owner, peers):
    return owner ^ me if peers & (peers - 1) == 0 else lax.rem(owner - me + peers, peers)


def hop_pairs(hop, peers):
    return [(i, i ^ hop if peers & (peers - 1) == 0 else (i + hop) % peers) for i in range(peers)]


def one_hot(keys, count):
    place = lax.broadcasted_iota(jnp.int32, (count, keys.shape[1]), 0)
    return jnp.where(place == keys, 1.0, 0.0).astype(jnp.bfloat16)


def slot_ranks(rel, group, rows_dev):
    f32, bf16 = jnp.float32, jnp.bfloat16
    per_owner = rows_dev // LANES
    high = rel >> 7
    low = rel & (LANES - 1)
    high_hot = one_hot(high, group * per_owner)
    low_hot = one_hot(low, LANES)
    counts = lax.dot_general(high_hot, low_hot, (((1,), (1,)), ((), ())), preferred_element_type=f32)
    present = jnp.where(counts > 0.0, 1.0, 0.0).astype(bf16)
    from_lane = lax.broadcasted_iota(jnp.int32, (LANES, LANES), 0)
    to_lane = lax.broadcasted_iota(jnp.int32, (LANES, LANES), 1)
    before = jnp.where(from_lane < to_lane, 1.0, 0.0).astype(bf16)
    within = jnp.dot(present, before, preferred_element_type=f32)
    totals = jnp.dot(present, jnp.ones((LANES, LANES), bf16), preferred_element_type=f32).astype(bf16)
    span = lax.broadcasted_iota(jnp.int32, (per_owner, per_owner), 0)
    other = lax.broadcasted_iota(jnp.int32, (per_owner, per_owner), 1)
    earlier = jnp.where(other < span, 1.0, 0.0).astype(bf16)
    offsets = [
        jnp.dot(earlier, totals[o * per_owner : (o + 1) * per_owner], preferred_element_type=f32)
        for o in range(group)
    ]
    ranks = within + jnp.concatenate(offsets, axis=0)
    by_low = jnp.dot(ranks.T.astype(bf16), high_hot, preferred_element_type=f32)
    return jnp.sum(by_low * low_hot.astype(f32), axis=0, keepdims=True).astype(jnp.int32)


def pack_group(rel, rank, wide, first, outs, rows_dev, room):
    f32 = jnp.float32
    group = len(outs)
    strips = strip_rows(room)
    lane = lax.broadcasted_iota(jnp.int32, (room, LANES), 1)
    meta = jnp.zeros((room, LANES), f32)
    for o in range(group):
        inside = jnp.logical_and(rel >= (first + o) * rows_dev, rel < (first + o + 1) * rows_dev)
        match = one_hot(jnp.where(inside, rank, -1), room)
        summed = jnp.dot(match, wide, preferred_element_type=f32)
        sums = summed[:, :LANES]
        digit_high = summed[:, LANES : LANES + 1]
        digit_low = summed[:, LANES + 1 : LANES + 2]
        number = summed[:, LANES + 2 : LANES + 3]
        mark = jnp.where(
            number > 0.0,
            jnp.floor((digit_high * LANES + digit_low) / jnp.maximum(number, 1.0) + 0.5),
            float(rows_dev),
        )
        largest = jnp.max(jnp.abs(sums), axis=1, keepdims=True)
        power = jnp.ceil(jnp.log2(jnp.maximum(largest, 1e-30) * (1.0 / TOP)))
        code = jnp.clip(jnp.round(sums * jnp.exp2(-power)), -TOP, TOP)
        outs[o][:room, :] = code.astype(jnp.int32).astype(jnp.int16)
        meta = jnp.where(lane == 2 * o, mark, jnp.where(lane == 2 * o + 1, power, meta))
    flat = meta.T.astype(jnp.int32)
    for o in range(group):
        rows = []
        for k in range(2):
            for c in range(strips):
                piece = flat[2 * o + k : 2 * o + k + 1, c * LANES : min((c + 1) * LANES, room)]
                if piece.shape[1] < LANES:
                    piece = jnp.concatenate([piece, jnp.zeros((1, LANES - piece.shape[1]), jnp.int32)], axis=1)
                rows.append(piece)
        rows.append(jnp.zeros((META - len(rows), LANES), jnp.int32))
        outs[o][room:, :] = jnp.concatenate(rows, axis=0).astype(jnp.int16)


def low_part(ids, size):
    return ids & (size - 1) if size & (size - 1) == 0 else lax.rem(ids, size)


def relative_rows(ids, peers, rows_dev):
    me = lax.axis_index("dp")
    if rows_dev & (rows_dev - 1) == 0 and peers & (peers - 1) == 0:
        return ids ^ (me * rows_dev)
    owner = ids // rows_dev
    return relative(me, owner, peers) * rows_dev + (ids - owner * rows_dev)


def pack_far_kernel(peers, rows_dev, room, ids_hbm, grads_hbm, table_hbm, first_hbm, *refs):
    far = peers - peers // 2
    outs, refs = refs[:far], refs[far:]
    rel_ref, rank_ref, wide_ref, table_ref, first_ref, ids_ref, grads_ref, sems = refs
    pairs = ((ids_hbm, ids_ref), (grads_hbm, grads_ref), (table_hbm, table_ref), (first_hbm, first_ref))
    copies = [pltpu.make_async_copy(a, b, sems.at[n]) for n, (a, b) in enumerate(pairs)]
    for copy in copies:
        copy.start()
    copies[0].wait()
    rel = relative_rows(ids_ref[...], peers, rows_dev)
    tok = rel.shape[1]
    rank = slot_ranks(rel, peers, rows_dev)
    rel_ref[...] = rel
    rank_ref[...] = rank
    sub = lax.broadcasted_iota(jnp.int32, (8, tok), 0)
    high = low_part(rel, rows_dev) >> 7
    low = rel & (LANES - 1)
    digits = jnp.where(sub == 0, high, jnp.where(sub == 1, low, jnp.where(sub == 2, 1, 0))).astype(jnp.float32)
    aux = []
    for c in range(tok // LANES):
        tile = digits[:, c * LANES : (c + 1) * LANES]
        tile = jnp.concatenate([tile, jnp.zeros((LANES - 8, LANES), jnp.float32)], axis=0)
        aux.append(tile.T)
    copies[1].wait()
    wide = jnp.concatenate([grads_ref[...], jnp.concatenate(aux, axis=0).astype(jnp.bfloat16)], axis=1)
    wide_ref[...] = wide
    pack_group(rel, rank, wide, peers // 2, outs, rows_dev, room)
    for copy in copies[2:]:
        copy.wait()


def pack_near_kernel(peers, rows_dev, room, rel_ref, rank_ref, wide_ref, second_hbm, *refs):
    outs, (second_ref, sem) = refs[: peers // 2], refs[peers // 2 :]
    copy = pltpu.make_async_copy(second_hbm, second_ref, sem)
    copy.start()
    pack_group(rel_ref[...], rank_ref[...], wide_ref[...], 0, outs, rows_dev, room)
    copy.wait()


def open_blocks(got, room, marks_buf, slots, sem, wide):
    strips = strip_rows(room)
    f32, bf16 = jnp.float32, jnp.bfloat16
    lines = len(got) * strips
    strip = min(room, LANES)
    mark_rows, power_rows = [], []
    for ref in got:
        meta = ref[room:, :].astype(jnp.int32)
        mark_rows.append(meta[0:strips])
        power_rows.append(meta[strips : 2 * strips])
    marks = jnp.concatenate(mark_rows, axis=0)
    marks_buf[...] = marks
    copy = pltpu.make_async_copy(marks_buf, slots, sem)
    copy.start()
    fill = jnp.zeros((LANES - 2 * lines, LANES), jnp.int32)
    both = jnp.concatenate([marks] + power_rows + [fill], axis=0).astype(f32)
    columns = both.T
    mark_columns = columns.astype(jnp.int32)
    scale_columns = jnp.exp2(columns)
    mark_line = jnp.concatenate([marks[k : k + 1, :strip] for k in range(lines)], axis=1)
    power_line = jnp.concatenate([both[lines + k : lines + k + 1, :strip] for k in range(lines)], axis=1)
    scale_line = jnp.exp2(power_line)
    for s, ref in enumerate(got):
        code = ref[:room, :].astype(jnp.int32)
        upper = (code + 128) >> 8
        lower = code - upper * 256
        halves = jnp.concatenate([upper.astype(f32), lower.astype(f32)], axis=1)
        wide[s * room : (s + 1) * room, :] = halves.astype(bf16)
    return copy, lines, strip, mark_line, scale_line, mark_columns, scale_columns


def block_sums(block, strip, mark_line, scale_line, mark_columns, wide):
    same = [
        jnp.where(mark_columns[:strip, k : k + 1] == mark_line, scale_line, 0.0).astype(jnp.bfloat16) for k in block
    ]
    sums = jnp.dot(jnp.concatenate(same, axis=0), wide[...], preferred_element_type=jnp.float32)
    return sums[:, :LANES] * 256.0 + sums[:, LANES:]


def own_rows(k, strip, lines, scale_columns, wide):
    own = wide[k * strip : (k + 1) * strip, :].astype(jnp.float32)
    return (own[:, :LANES] * 256.0 + own[:, LANES:]) * scale_columns[:strip, lines + k : lines + k + 1]


def fold(product):
    return jnp.sum(product.reshape(product.shape[0] // 8, 8, LANES), axis=0)


def line_blocks(lines, strip):
    per_block = max(1, 256 // strip)
    return [range(k, min(k + per_block, lines)) for k in range(0, lines, per_block)]


def join_kernel(group, room, opens, ends, *refs):
    got, refs = refs[:group], refs[group:]
    if not opens:
        (_, sum_ref), refs = refs[:2], refs[2:]
    grad_ref, part_ref, wide, sums_buf, before_buf, marks_buf, slots, sem = refs
    if opens:
        grad_ref[...] = jnp.zeros_like(grad_ref)
    copy, lines, strip, mark_line, scale_line, mark_columns, scale_columns = open_blocks(
        got, room, marks_buf, slots, sem, wide
    )
    total = jnp.zeros((8, LANES), jnp.float32) if opens else sum_ref[...]
    if not opens:
        copy.wait()
        for k in range(lines):
            for r in range(strip):
                before_buf[k * strip + r : k * strip + r + 1, :] = grad_ref[pl.ds(slots[k, r], 1), :]
    for block in line_blocks(lines, strip):
        sums = block_sums(block, strip, mark_line, scale_line, mark_columns, wide)
        for n, k in enumerate(block):
            here = slice(k * strip, (k + 1) * strip)
            after = sums[n * strip : (n + 1) * strip]
            twice = after
            if not opens:
                before = before_buf[here, :]
                after = before + after
                twice = before + after
            sums_buf[here, :] = after
            total = total + fold(own_rows(k, strip, lines, scale_columns, wide) * twice)
        if opens and block[0] == 0:
            copy.wait()
        for k in block:
            for r in range(strip):
                grad_ref[pl.ds(slots[k, r], 1), :] = sums_buf[k * strip + r : k * strip + r + 1, :]
    if ends:
        total = jnp.sum(total, axis=0, keepdims=True)
        total = jnp.sum(total, axis=1, keepdims=True)
        part_ref[...] = jnp.broadcast_to(total[None], part_ref.shape)
    else:
        part_ref[...] = total


def update_kernel(limit, step, parts_ref, grad_ref, table_ref, first_ref, second_ref, table_out, first_out, second_out,
                  table_buf, first_buf, second_buf, sems):
    total = jnp.sum(parts_ref[...], axis=0)
    scale = limit / jnp.maximum(jnp.sqrt(total), limit)
    rows = table_ref.shape[0]
    copies = []
    for n in range(rows // step):
        part = pl.ds(n * step, step)
        clipped = scale * grad_ref[part, :]
        new_first = beta_first * first_ref[part, :] + (1.0 - beta_first) * clipped
        first_buf[part, :] = new_first
        new_second = beta_second * second_ref[part, :] + (1.0 - beta_second) * clipped * clipped
        second_buf[part, :] = new_second
        change = (new_first * (learn_rate / first_fix)) / (jnp.sqrt(new_second * (1.0 / second_fix)) + adam_eps)
        table_buf[part, :] = table_ref[part, :] * (1.0 - learn_rate * decay_rate) - change
        for k, (a, b) in enumerate(((first_buf, first_out), (second_buf, second_out), (table_buf, table_out))):
            copy = pltpu.make_async_copy(a.at[part], b.at[part], sems.at[k, n])
            copy.start()
            copies.append(copy)
    for copy in copies:
        copy.wait()


def body(table, first_moment, second_moment, grads, ids):
    peers = lax.axis_size("dp")
    everyone = peers * lax.axis_size("mp")
    rows_dev, width = table.shape
    tok_dev = grads.shape[0]
    room = tok_dev // peers
    strips = strip_rows(room)
    f32 = jnp.float32
    shape = jax.ShapeDtypeStruct
    vmem = pl.BlockSpec(memory_space=pltpu.VMEM)
    hbm = pl.BlockSpec(memory_space=pltpu.HBM)
    in_hbm = lambda x: pltpu.with_memory_space_constraint(x, pltpu.HBM)
    in_vmem = lambda x: pltpu.with_memory_space_constraint(x, pltpu.VMEM)
    kept = pltpu.VMEM((rows_dev, width), f32)
    dense = shape((rows_dev, width), f32)
    parcel = shape((room + META, width), jnp.int16)
    params = lambda mib: pltpu.CompilerParams(vmem_limit_bytes=mib * MIB)
    effort = lambda flops, moved: pl.CostEstimate(flops=flops, bytes_accessed=moved, transcendentals=0)
    near, far = peers // 2, peers - peers // 2
    line = pltpu.VMEM((1, tok_dev), jnp.int32)
    *packed_far, rel, rank, wide, table_kept, first_kept = pl.pallas_call(
        functools.partial(pack_far_kernel, peers, rows_dev, room),
        out_shape=(parcel,) * far
        + (line, line, pltpu.VMEM((tok_dev, 2 * width), jnp.bfloat16), kept, kept),
        in_specs=[hbm] * 4,
        out_specs=(vmem,) * (far + 5),
        scratch_shapes=[
            pltpu.VMEM((1, tok_dev), jnp.int32),
            pltpu.VMEM((tok_dev, width), jnp.bfloat16),
            pltpu.SemaphoreType.DMA((4,)),
        ],
        compiler_params=params(24),
        name="pack_far",
    )(*[in_hbm(x) for x in (ids.reshape(1, tok_dev), grads, table, first_moment)])
    got = [None] * peers
    for hop in range(peers - 1, near - 1, -1):
        got[hop] = lax.ppermute(packed_far[hop - near], "dp", hop_pairs(hop, peers))
    *packed_near, second_kept = pl.pallas_call(
        functools.partial(pack_near_kernel, peers, rows_dev, room),
        out_shape=(parcel,) * near + (kept,),
        in_specs=[vmem, vmem, vmem, hbm],
        out_specs=(vmem,) * (near + 1),
        scratch_shapes=[pltpu.SemaphoreType.DMA],
        compiler_params=params(24),
        cost_estimate=effort(4 * tok_dev * near * room * width, 16 * rows_dev * width),
        name="pack_near",
    )(in_vmem(rel), in_vmem(rank), in_vmem(wide), in_hbm(second_moment))
    got[0] = packed_near[0]
    for hop in range(near - 1, 0, -1):
        got[hop] = lax.ppermute(packed_near[hop], "dp", hop_pairs(hop, peers))
    longer = pltpu.VMEM((rows_dev + 8, width), f32)

    half, most = far // 2, 3 * far // 4
    hops = list(range(peers - 1, 0, -1))
    rounds = [[0, *hops[:half]], [*hops[half:most], *hops[far:]], hops[most:far]]
    grad_rows = part = None
    for n, members in enumerate(rounds):
        opens, ends = n == 0, n == len(rounds) - 1
        group = len(members)
        grad_rows, part = pl.pallas_call(
            functools.partial(join_kernel, group, room, opens, ends),
            out_shape=(longer, shape((everyone, 1, width) if ends else (8, LANES), f32)),
            in_specs=[vmem] * (group if opens else group + 2),
            out_specs=(vmem,) * 2,
            input_output_aliases={} if opens else {group: 0},
            scratch_shapes=[
                pltpu.VMEM((group * room, 2 * width), jnp.bfloat16),
                pltpu.VMEM((group * room, width), f32),
                pltpu.VMEM((group * room, width), f32),
                pltpu.VMEM((group * strips, LANES), jnp.int32),
                pltpu.SMEM((group * strips, LANES), jnp.int32),
                pltpu.SemaphoreType.DMA,
            ],
            compiler_params=params(16),
            cost_estimate=effort(width, width),
            name="join_rows_%d" % n,
        )(*[got[hop] for hop in members], *(() if opens else (in_vmem(grad_rows), part)))
    parts = lax.all_to_all(part, ("dp", "mp"), split_axis=0, concat_axis=0, tiled=True)
    limit = math.sqrt(tok_dev * everyone * width)
    step = math.gcd(1024, rows_dev)
    return pl.pallas_call(
        functools.partial(update_kernel, limit, step),
        out_shape=(dense,) * 3,
        in_specs=[vmem] * 5,
        out_specs=(hbm,) * 3,
        scratch_shapes=[pltpu.VMEM((rows_dev, width), f32)] * 3 + [pltpu.SemaphoreType.DMA((3, rows_dev // step))],
        compiler_params=params(20),
        name="update_rows",
    )(parts, *[in_vmem(x) for x in (grad_rows, table_kept, first_kept, second_kept)])


def solution(mesh):
    in_specs = (P("dp", "mp"), P("dp", "mp"), P("dp", "mp"), P("dp", "mp"), P("dp"))
    out_specs = (P("dp", "mp"), P("dp", "mp"), P("dp", "mp"))
    return jax.shard_map(body, mesh=mesh, in_specs=in_specs, out_specs=out_specs, check_vma=False)
```

time: 47.5 us -> 44.7 us (0.941)
  waiting for transfers between devices: 4.72 us -> 0.02 us
  starting transfers between devices: 13.3 us -> 15.8 us
  blocking collectives: 12.6 us -> 10.6 us
  Pallas kernels: 15.9 us -> 17.2 us
    ppermute x7, waiting for transfers between devices: 4.72 us -> 0.02 us  [the longest x4 0.01 us: body(): got[hop] = lax.ppermute(packed_far[hop - near], 'dp', hop_pairs(hop, peers))]
    ppermute x7, starting transfers between devices: 13.3 us -> 15.8 us  [the longest x4 12.2 us: body(): got[hop] = lax.ppermute(packed_far[hop - near], 'dp', hop_pairs(hop, peers))]
    all_to_all x1, blocking collectives: 12.6 us -> 10.6 us  [body(): lax.all_to_all(part, ('dp', 'mp'), split_axis=0, concat_axis=0, tiled=True)]
    pallas_call x2 -> x5, Pallas kernels: 10.7 us -> 12 us  [the longest x1 5.12 us: body(): pl.pallas_call(functools.partial(pack_far_kernel, peers, rows_dev, room),...]
  transfers between devices with their start and end apart: 7 -> 7, of which waited for: 3 -> 0; matrix products, arithmetic and copies ran while one was open for 0% -> 0% of each run, Pallas kernels for 0% -> 13%
where the time goes in v3:
time: 44.7 us; the launch traced here: 44.5 us
  Pallas kernels  17.2 us (38%)
  starting transfers between devices  15.8 us (35%)
  blocking collectives  10.6 us (24%)
  between operations  0.88 us (2%)
    ppermute x4, starting transfers between devices, body(): got[hop] = lax.ppermute(packed_far[hop - near], 'dp', hop_pairs(hop, peers))  12.2 us
    all_to_all x1, blocking collectives, body(): lax.all_to_all(part, ('dp', 'mp'), split_axis=0, concat_axis=0, tiled=True)  10.6 us
    pallas_call x1, Pallas kernels, body(): pl.pallas_call(functools.partial(update_kernel, limit, step), out_shape=(...  5.28 us
    pallas_call x1, Pallas kernels, body(): pl.pallas_call(functools.partial(pack_far_kernel, peers, rows_dev, room),...  5.12 us
    pallas_call x3, Pallas kernels, body(): pl.pallas_call(functools.partial(join_kernel, group, room, opens, ends),...  4.58 us
    ppermute x3, starting transfers between devices, body(): got[hop] = lax.ppermute(packed_near[hop], 'dp', hop_pairs(hop, peers))  3.55 us
    pallas_call x1, Pallas kernels, body(): pl.pallas_call(functools.partial(pack_near_kernel, peers, rows_dev, room)...  2.26 us
  transfers between devices with their start and end apart: 7, of which 0 were waited for; matrix products, arithmetic and copies ran while one was open for 0% of the time, Pallas kernels for 13%

profile of v3, /device:TPU:0, one launch (start us, length us, event | category | flops | bytes accessed | tf_op | source)
XLA Modules:
  0.0 44.5 jit_solution(12859365820686651865)
XLA Ops:
  0.6 5.1 %pack_far.1 = (s16[272,128]{1,0:T(8,128)(2,1)S(1)}, s16[272,128]{1,0:T(8,128)(2,1)S(1)}, s16[272,128]{1,0:T(8,128)(2,1)S(1)}, s16[272,128]{1,0:T(8,128)(2,1)S(1)...) custom-call(s32[1,2048]{1,0:T(1,128)} %bitcast.1, ...), custom_call_target="tpu_custom_call" | custom-call | tf_op jit(solution)/shard_map/pack_far/pallas_call | solution.py:293
  5.8 5.1 %collective-permute-start.1 = (s16[272,128]{1,0:T(8,128)(2,1)S(1)}, s16[272,128]{1,0:T(8,128)(2,1)S(1)}, u32[]{:S(2)}, u32[]{:S(2)}) collective-permute-start(s16[272,128]{1,0:T(8,128)(2,1)S(1)} %get-tuple-element.24), channel_id=1, source_target_pairs={{0,20},{4,16},{8,28},{12,24},{16,4},{20,0},{24,12},{28,8},{1,21},{... | collective-permute-start | bytes 208904 | tf_op jit(solution)/shard_map/ppermute | solution.py:309
  10.8 1.3 %collective-permute-start.5 = (s16[272,128]{1,0:T(8,128)(2,1)S(1)}, s16[272,128]{1,0:T(8,128)(2,1)S(1)}, u32[]{:S(2)}, u32[]{:S(2)}) collective-permute-start(s16[272,128]{1,0:T(8,128)(2,1)S(1)} %get-tuple-element.32), channel_id=1, source_target_pairs={{0,28},{4,24},{8,20},{12,16},{16,12},{20,8},{24,4},{28,0},{1,29},{... | collective-permute-start | bytes 208904 | tf_op jit(solution)/shard_map/ppermute | solution.py:309
  12.1 2.5 %collective-permute-start.6 = (s16[272,128]{1,0:T(8,128)(2,1)S(1)}, s16[272,128]{1,0:T(8,128)(2,1)S(1)}, u32[]{:S(2)}, u32[]{:S(2)}) collective-permute-start(s16[272,128]{1,0:T(8,128)(2,1)S(1)} %get-tuple-element.33), channel_id=1, source_target_pairs={{0,24},{4,28},{8,16},{12,20},{16,8},{20,12},{24,0},{28,4},{1,25},{... | collective-permute-start | bytes 208904 | tf_op jit(solution)/shard_map/ppermute | solution.py:309
  14.6 2.3 %pack_near.1 = (s16[272,128]{1,0:T(8,128)(2,1)S(1)}, s16[272,128]{1,0:T(8,128)(2,1)S(1)}, s16[272,128]{1,0:T(8,128)(2,1)S(1)}, s16[272,128]{1,0:T(8,128)(2,1)S(1)}, f32[8192,128]{1,0:T(8,128)S(1)}) custom-call(s32[1,2048]{1,0:T(1,128)S(1)} %get-tuple-element.25.rel_ref, s32[1,2048]{1,0:T(1,128)S(1)} %get-tuple-element.26.rank_ref, ...), custom_call_target="tpu_custom_call" | custom-call | flops 1073741824 | bytes 16777216 | tf_op jit(solution)/shard_map/pack_near/pallas_call | solution.py:310
  16.9 0.8 %collective-permute-start.2 = (s16[272,128]{1,0:T(8,128)(2,1)S(1)}, s16[272,128]{1,0:T(8,128)(2,1)S(1)}, u32[]{:S(2)}, u32[]{:S(2)}) collective-permute-start(s16[272,128]{1,0:T(8,128)(2,1)S(1)} %get-tuple-element.28), channel_id=1, source_target_pairs={{0,12},{4,8},{8,4},{12,0},{16,28},{20,24},{24,20},{28,16},{1,13},{... | collective-permute-start | bytes 208904 | tf_op jit(solution)/shard_map/ppermute | solution.py:322
  17.7 2.2 %collective-permute-start.3 = (s16[272,128]{1,0:T(8,128)(2,1)S(1)}, s16[272,128]{1,0:T(8,128)(2,1)S(1)}, u32[]{:S(2)}, u32[]{:S(2)}) collective-permute-start(s16[272,128]{1,0:T(8,128)(2,1)S(1)} %get-tuple-element.29), channel_id=1, source_target_pairs={{0,8},{4,12},{8,0},{12,4},{16,24},{20,28},{24,16},{28,20},{1,9},{5... | collective-permute-start | bytes 208904 | tf_op jit(solution)/shard_map/ppermute | solution.py:322
  19.9 0.0 collective-permute-done.5.refs_1_
  19.9 0.5 %collective-permute-start.4 = (s16[272,128]{1,0:T(8,128)(2,1)S(1)}, s16[272,128]{1,0:T(8,128)(2,1)S(1)}, u32[]{:S(2)}, u32[]{:S(2)}) collective-permute-start(s16[272,128]{1,0:T(8,128)(2,1)S(1)} %get-tuple-element.30), channel_id=1, source_target_pairs={{0,4},{4,0},{8,12},{12,8},{16,20},{20,16},{24,28},{28,24},{1,5},{5... | collective-permute-start | bytes 208904 | tf_op jit(solution)/shard_map/ppermute | solution.py:322
  20.4 0.0 collective-permute-done.6.refs_2_
  20.4 3.4 %collective-permute-start = (s16[272,128]{1,0:T(8,128)(2,1)S(1)}, s16[272,128]{1,0:T(8,128)(2,1)S(1)}, u32[]{:S(2)}, u32[]{:S(2)}) collective-permute-start(s16[272,128]{1,0:T(8,128)(2,1)S(1)} %get-tuple-element.23), channel_id=1, source_target_pairs={{0,16},{4,20},{8,24},{12,28},{16,0},{20,4},{24,8},{28,12},{1,17},{... | collective-permute-start | bytes 208904 | tf_op jit(solution)/shard_map/ppermute | solution.py:309
  23.8 1.3 %join_rows_0.1 = (f32[8200,128]{1,0:T(8,128)S(1)}, f32[8,128]{1,0:T(8,128)S(1)}) custom-call(s16[272,128]{1,0:T(8,128)(2,1)S(1)} %get-tuple-element.31.refs_0_, s16[272,128]{1,0:T(8,128)(2,1)S(1)} %collective-permute-done.5.refs_1_, s16[272,128]{1,0:T(8,128)(2,1)S(1)} %collective-permute-done.6.refs_2_), custom_call_target="tpu_custom_call" | custom-call | flops 128 | bytes 128 | tf_op jit(solution)/shard_map/join_rows_0/pallas_call | solution.py:332
  25.2 0.0 collective-permute-done.1.refs_0_
  25.2 0.0 collective-permute-done.2.refs_1_
  25.2 0.0 collective-permute-done.3.refs_2_
  25.2 0.0 collective-permute-done.4.refs_3_
  25.2 2.2 %join_rows_1.1 = (f32[8200,128]{1,0:T(8,128)S(1)}, f32[8,128]{1,0:T(8,128)S(1)}) custom-call(s16[272,128]{1,0:T(8,128)(2,1)S(1)} %collective-permute-done.1.refs_0_, s16[272,128]{1,0:T(8,128)(2,1)S(1)} %collective-permute-done.2.refs_1_, s16[272,128]{1,0:T(8,128)(2,1)S(1)} %collective-permute-done.3.refs_2_, ...), custom_call_target="tpu_custom_call", output_to_operand_aliasing={{0}: (4, {})} | custom-call | flops 128 | bytes 128 | tf_op jit(solution)/shard_map/join_rows_1/pallas_call | solution.py:332
  27.5 0.0 collective-permute-done.refs_0_
  27.5 1.0 %join_rows_2.1 = (f32[8200,128]{1,0:T(8,128)S(1)}, f32[32,1,128]{2,1,0:T(1,128)S(1)}) custom-call(s16[272,128]{1,0:T(8,128)(2,1)S(1)} %collective-permute-done.refs_0_, f32[8200,128]{1,0:T(8,128)S(1)} %get-tuple-element.36.refs_1_, f32[8,128]{1,0:T(8,128)S(1)} %get-tuple-element.37.refs_2_), custom_call_target="tpu_custom_call", output_to_operand_aliasing={{0}: (1, {})} | custom-call | flops 128 | bytes 128 | tf_op jit(solution)/shard_map/join_rows_2/pallas_call | solution.py:332
  28.5 10.6 %all_to_all.5.parts_ref = f32[32,1,128]{2,1,0:T(1,128)S(1)} all-to-all(f32[32,1,128]{2,1,0:T(1,128)S(1)} %get-tuple-element.38), channel_id=1, replica_groups=mesh['dp'=8,'mp'=4] {'dp','mp'}, dimensions={0} | all-to-all | bytes 32768 | tf_op jit(solution)/shard_map/all_to_all | solution.py:350
  39.1 5.3 %update_rows.1 = (f32[8192,128]{1,0:T(8,128)}, f32[8192,128]{1,0:T(8,128)}, f32[8192,128]{1,0:T(8,128)}) custom-call(f32[32,1,128]{2,1,0:T(1,128)S(1)} %all_to_all.5.parts_ref, f32[8200,128]{1,0:T(8,128)S(1)} %get-tuple-element.39.grad_ref, f32[8192,128]{1,0:T(8,128)S(1)} %get-tuple-element.40.table_ref, f32[8192,128]{1,0:T(8,128)S(1)} %get-tuple-element.41.first_ref, ...), custom_call_target="tpu_custom_call" | custom-call | tf_op jit(solution)/shard_map/update_rows/pallas_call | solution.py:353
Async XLA Ops:
  5.8 19.4 %collective-permute-start.1 = (s16[272,128]{1,0:T(8,128)(2,1)S(1)}, s16[272,128]{1,0:T(8,128)(2,1)S(1)}, u32[]{:S(2)}, u32[]{:S(2)}) collective-permute-start(s16[272,128]{1,0:T(8,128)(2,1)S(1)} %get-tuple-element.24), channel_id=1, source_target_pairs={{0,20},{4,16},{8,28},{12,24},{16,4},{20,0},{24,12},{28,8},{1,21},{... | collective-permute-start | bytes 208904 | tf_op jit(solution)/shard_map/ppermute | solution.py:309
  10.8 9.1 %collective-permute-start.5 = (s16[272,128]{1,0:T(8,128)(2,1)S(1)}, s16[272,128]{1,0:T(8,128)(2,1)S(1)}, u32[]{:S(2)}, u32[]{:S(2)}) collective-permute-start(s16[272,128]{1,0:T(8,128)(2,1)S(1)} %get-tuple-element.32), channel_id=1, source_target_pairs={{0,28},{4,24},{8,20},{12,16},{16,12},{20,8},{24,4},{28,0},{1,29},{... | collective-permute-start | bytes 208904 | tf_op jit(solution)/shard_map/ppermute | solution.py:309
  12.1 8.3 %collective-permute-start.6 = (s16[272,128]{1,0:T(8,128)(2,1)S(1)}, s16[272,128]{1,0:T(8,128)(2,1)S(1)}, u32[]{:S(2)}, u32[]{:S(2)}) collective-permute-start(s16[272,128]{1,0:T(8,128)(2,1)S(1)} %get-tuple-element.33), channel_id=1, source_target_pairs={{0,24},{4,28},{8,16},{12,20},{16,8},{20,12},{24,0},{28,4},{1,25},{... | collective-permute-start | bytes 208904 | tf_op jit(solution)/shard_map/ppermute | solution.py:309
  16.9 8.3 %collective-permute-start.2 = (s16[272,128]{1,0:T(8,128)(2,1)S(1)}, s16[272,128]{1,0:T(8,128)(2,1)S(1)}, u32[]{:S(2)}, u32[]{:S(2)}) collective-permute-start(s16[272,128]{1,0:T(8,128)(2,1)S(1)} %get-tuple-element.28), channel_id=1, source_target_pairs={{0,12},{4,8},{8,4},{12,0},{16,28},{20,24},{24,20},{28,16},{1,13},{... | collective-permute-start | bytes 208904 | tf_op jit(solution)/shard_map/ppermute | solution.py:322
  17.7 7.5 %collective-permute-start.3 = (s16[272,128]{1,0:T(8,128)(2,1)S(1)}, s16[272,128]{1,0:T(8,128)(2,1)S(1)}, u32[]{:S(2)}, u32[]{:S(2)}) collective-permute-start(s16[272,128]{1,0:T(8,128)(2,1)S(1)} %get-tuple-element.29), channel_id=1, source_target_pairs={{0,8},{4,12},{8,0},{12,4},{16,24},{20,28},{24,16},{28,20},{1,9},{5... | collective-permute-start | bytes 208904 | tf_op jit(solution)/shard_map/ppermute | solution.py:322
  19.9 5.3 %collective-permute-start.4 = (s16[272,128]{1,0:T(8,128)(2,1)S(1)}, s16[272,128]{1,0:T(8,128)(2,1)S(1)}, u32[]{:S(2)}, u32[]{:S(2)}) collective-permute-start(s16[272,128]{1,0:T(8,128)(2,1)S(1)} %get-tuple-element.30), channel_id=1, source_target_pairs={{0,4},{4,0},{8,12},{12,8},{16,20},{20,16},{24,28},{28,24},{1,5},{5... | collective-permute-start | bytes 208904 | tf_op jit(solution)/shard_map/ppermute | solution.py:322
  20.4 7.0 %collective-permute-start = (s16[272,128]{1,0:T(8,128)(2,1)S(1)}, s16[272,128]{1,0:T(8,128)(2,1)S(1)}, u32[]{:S(2)}, u32[]{:S(2)}) collective-permute-start(s16[272,128]{1,0:T(8,128)(2,1)S(1)} %get-tuple-element.23), channel_id=1, source_target_pairs={{0,16},{4,20},{8,24},{12,28},{16,0},{20,4},{24,8},{28,12},{1,17},{... | collective-permute-start | bytes 208904 | tf_op jit(solution)/shard_map/ppermute | solution.py:309

commit v4 on v3

--- a/solution.py
+++ b/solution.py
@@ -35,33 +35,38 @@
 
 
 def one_hot(keys, count):
-    place = lax.broadcasted_iota(jnp.int32, (count, keys.shape[1]), 0)
-    return jnp.where(place == keys, 1.0, 0.0).astype(jnp.bfloat16)
-
-
-def slot_ranks(rel, group, rows_dev):
+    tall = 16 if count % 16 == 0 else count
+    place = lax.broadcasted_iota(jnp.int32, (tall, keys.shape[1]), 0).astype(jnp.int16)
+    keys = jnp.broadcast_to(keys, (tall, keys.shape[1])).astype(jnp.int16)
+    one, zero = jnp.ones(keys.shape, jnp.bfloat16), jnp.zeros(keys.shape, jnp.bfloat16)
+    return jnp.concatenate([jnp.where(place == keys - k, one, zero) for k in range(0, count, tall)], axis=0)
+
+
+def rank_tables(group, per_owner):
+    bf16 = jnp.bfloat16
+    row = lax.broadcasted_iota(jnp.int32, (LANES, LANES), 0)
+    column = lax.broadcasted_iota(jnp.int32, (LANES, LANES), 1)
+    before = jnp.where(column < row, 1.0, 0.0).astype(bf16)
+    ones = jnp.ones((LANES, LANES), bf16)
+    source = lax.broadcasted_iota(jnp.int32, (per_owner, per_owner), 0)
+    target = lax.broadcasted_iota(jnp.int32, (per_owner, per_owner), 1)
+    ahead = jnp.where(source < target, 1.0, 0.0)
+    blank = jnp.zeros((per_owner, per_owner), jnp.float32)
+    rows = [jnp.concatenate([ahead if k == o else blank for k in range(group)], axis=1) for o in range(group)]
+    return before, ones, jnp.concatenate(rows, axis=0).astype(bf16)
+
+
+def slot_ranks(rel, tables):
     f32, bf16 = jnp.float32, jnp.bfloat16
-    per_owner = rows_dev // LANES
-    high = rel >> 7
-    low = rel & (LANES - 1)
-    high_hot = one_hot(high, group * per_owner)
-    low_hot = one_hot(low, LANES)
-    counts = lax.dot_general(high_hot, low_hot, (((1,), (1,)), ((), ())), preferred_element_type=f32)
+    before, ones, ahead = tables
+    high_hot = one_hot(rel >> 7, ahead.shape[0])
+    low_hot = one_hot(rel & (LANES - 1), LANES)
+    counts = lax.dot_general(low_hot, high_hot, (((1,), (1,)), ((), ())), preferred_element_type=f32)
     present = jnp.where(counts > 0.0, 1.0, 0.0).astype(bf16)
-    from_lane = lax.broadcasted_iota(jnp.int32, (LANES, LANES), 0)
-    to_lane = lax.broadcasted_iota(jnp.int32, (LANES, LANES), 1)
-    before = jnp.where(from_lane < to_lane, 1.0, 0.0).astype(bf16)
-    within = jnp.dot(present, before, preferred_element_type=f32)
-    totals = jnp.dot(present, jnp.ones((LANES, LANES), bf16), preferred_element_type=f32).astype(bf16)
-    span = lax.broadcasted_iota(jnp.int32, (per_owner, per_owner), 0)
-    other = lax.broadcasted_iota(jnp.int32, (per_owner, per_owner), 1)
-    earlier = jnp.where(other < span, 1.0, 0.0).astype(bf16)
-    offsets = [
-        jnp.dot(earlier, totals[o * per_owner : (o + 1) * per_owner], preferred_element_type=f32)
-        for o in range(group)
-    ]
-    ranks = within + jnp.concatenate(offsets, axis=0)
-    by_low = jnp.dot(ranks.T.astype(bf16), high_hot, preferred_element_type=f32)
+    within = jnp.dot(before, present, preferred_element_type=f32)
+    totals = jnp.dot(ones, present, preferred_element_type=f32).astype(bf16)
+    ranks = within + jnp.dot(totals, ahead, preferred_element_type=f32)
+    by_low = jnp.dot(ranks.astype(bf16), high_hot, preferred_element_type=f32)
     return jnp.sum(by_low * low_hot.astype(f32), axis=0, keepdims=True).astype(jnp.int32)
 
 
@@ -114,18 +119,21 @@
     return relative(me, owner, peers) * rows_dev + (ids - owner * rows_dev)
 
 
-def pack_far_kernel(peers, rows_dev, room, ids_hbm, grads_hbm, table_hbm, first_hbm, *refs):
+def pack_far_kernel(peers, rows_dev, room, ids_hbm, grads_hbm, table_hbm, *refs):
     far = peers - peers // 2
     outs, refs = refs[:far], refs[far:]
-    rel_ref, rank_ref, wide_ref, table_ref, first_ref, ids_ref, grads_ref, sems = refs
-    pairs = ((ids_hbm, ids_ref), (grads_hbm, grads_ref), (table_hbm, table_ref), (first_hbm, first_ref))
+    rel_ref, rank_ref, wide_ref, table_ref, ids_ref, grads_ref, sems = refs
+    pairs = ((ids_hbm, ids_ref), (grads_hbm, grads_ref), (table_hbm, table_ref))
     copies = [pltpu.make_async_copy(a, b, sems.at[n]) for n, (a, b) in enumerate(pairs)]
-    for copy in copies:
+    copies[0].start()
+    copies[1].start()
+    tables = rank_tables(peers, rows_dev // LANES)
+    copies[0].wait()
+    for copy in copies[2:]:
         copy.start()
-    copies[0].wait()
     rel = relative_rows(ids_ref[...], peers, rows_dev)
     tok = rel.shape[1]
-    rank = slot_ranks(rel, peers, rows_dev)
+    rank = slot_ranks(rel, tables)
     rel_ref[...] = rel
     rank_ref[...] = rank
     sub = lax.broadcasted_iota(jnp.int32, (8, tok), 0)
@@ -210,7 +218,14 @@
     got, refs = refs[:group], refs[group:]
     if not opens:
         (_, sum_ref), refs = refs[:2], refs[2:]
-    grad_ref, part_ref, wide, sums_buf, before_buf, marks_buf, slots, sem = refs
+    middle = not opens and not ends
+    if middle:
+        state_hbm, grad_ref, part_ref, state_ref, *refs, state_sem = refs
+        state_copy = pltpu.make_async_copy(state_hbm, state_ref, state_sem)
+        state_copy.start()
+    else:
+        grad_ref, part_ref, *refs = refs
+    wide, sums_buf, before_buf, marks_buf, slots, sem = refs
     if opens:
         grad_ref[...] = jnp.zeros_like(grad_ref)
     copy, lines, strip, mark_line, scale_line, mark_columns, scale_columns = open_blocks(
@@ -245,6 +260,8 @@
         part_ref[...] = jnp.broadcast_to(total[None], part_ref.shape)
     else:
         part_ref[...] = total
+    if middle:
+        state_copy.wait()
 
 
 def update_kernel(limit, step, parts_ref, grad_ref, table_ref, first_ref, second_ref, table_out, first_out, second_out,
@@ -290,20 +307,20 @@
     effort = lambda flops, moved: pl.CostEstimate(flops=flops, bytes_accessed=moved, transcendentals=0)
     near, far = peers // 2, peers - peers // 2
     line = pltpu.VMEM((1, tok_dev), jnp.int32)
-    *packed_far, rel, rank, wide, table_kept, first_kept = pl.pallas_call(
+    *packed_far, rel, rank, wide, table_kept = pl.pallas_call(
         functools.partial(pack_far_kernel, peers, rows_dev, room),
         out_shape=(parcel,) * far
-        + (line, line, pltpu.VMEM((tok_dev, 2 * width), jnp.bfloat16), kept, kept),
-        in_specs=[hbm] * 4,
-        out_specs=(vmem,) * (far + 5),
+        + (line, line, pltpu.VMEM((tok_dev, 2 * width), jnp.bfloat16), kept),
+        in_specs=[hbm] * 3,
+        out_specs=(vmem,) * (far + 4),
         scratch_shapes=[
             pltpu.VMEM((1, tok_dev), jnp.int32),
             pltpu.VMEM((tok_dev, width), jnp.bfloat16),
-            pltpu.SemaphoreType.DMA((4,)),
+            pltpu.SemaphoreType.DMA((3,)),
         ],
         compiler_params=params(24),
         name="pack_far",
-    )(*[in_hbm(x) for x in (ids.reshape(1, tok_dev), grads, table, first_moment)])
+    )(*[in_hbm(x) for x in (ids.reshape(1, tok_dev), grads, table)])
     got = [None] * peers
     for hop in range(peers - 1, near - 1, -1):
         got[hop] = lax.ppermute(packed_far[hop - near], "dp", hop_pairs(hop, peers))
@@ -328,12 +345,18 @@
     grad_rows = part = None
     for n, members in enumerate(rounds):
         opens, ends = n == 0, n == len(rounds) - 1
+        middle = not opens and not ends
         group = len(members)
-        grad_rows, part = pl.pallas_call(
+        operands = [got[hop] for hop in members]
+        if not opens:
+            operands += [in_vmem(grad_rows), part]
+        if middle:
+            operands.append(in_hbm(first_moment))
+        grad_rows, part, *state = pl.pallas_call(
             functools.partial(join_kernel, group, room, opens, ends),
-            out_shape=(longer, shape((everyone, 1, width) if ends else (8, LANES), f32)),
-            in_specs=[vmem] * (group if opens else group + 2),
-            out_specs=(vmem,) * 2,
+            out_shape=(longer, shape((everyone, 1, width) if ends else (8, LANES), f32)) + (kept,) * middle,
+            in_specs=[vmem] * (len(operands) - middle) + [hbm] * middle,
+            out_specs=(vmem,) * (2 + middle),
             input_output_aliases={} if opens else {group: 0},
             scratch_shapes=[
                 pltpu.VMEM((group * room, 2 * width), jnp.bfloat16),
@@ -342,11 +365,14 @@
                 pltpu.VMEM((group * strips, LANES), jnp.int32),
                 pltpu.SMEM((group * strips, LANES), jnp.int32),
                 pltpu.SemaphoreType.DMA,
-            ],
+            ]
+            + [pltpu.SemaphoreType.DMA] * middle,
             compiler_params=params(16),
             cost_estimate=effort(width, width),
             name="join_rows_%d" % n,
-        )(*[got[hop] for hop in members], *(() if opens else (in_vmem(grad_rows), part)))
+        )(*operands)
+        if middle:
+            (first_kept,) = state
     parts = lax.all_to_all(part, ("dp", "mp"), split_axis=0, concat_axis=0, tiled=True)
     limit = math.sqrt(tok_dev * everyone * width)
     step = math.gcd(1024, rows_dev)

time: 44.7 us -> 44.4 us (level)
    pallas_call x1, Pallas kernels: 5.12 us -> 4.6 us  [body(): pl.pallas_call(functools.partial(pack_far_kernel, peers, rows_dev, room),...]
  transfers between devices with their start and end apart: 7 -> 7, of which waited for: 0 -> 0; matrix products, arithmetic and copies ran while one was open for 0% -> 0% of each run, Pallas kernels for 13% -> 14%
where the time goes in v4:
time: 44.4 us; the launch traced here: 44.1 us
  Pallas kernels  16.9 us (38%)
  starting transfers between devices  15.8 us (36%)
  blocking collectives  10.6 us (24%)
  between operations  0.88 us (2%)
    ppermute x4, starting transfers between devices, body(): got[hop] = lax.ppermute(packed_far[hop - near], 'dp', hop_pairs(hop, peers))  12.2 us
    all_to_all x1, blocking collectives, body(): lax.all_to_all(part, ('dp', 'mp'), split_axis=0, concat_axis=0, tiled=True)  10.6 us
    pallas_call x1, Pallas kernels, body(): pl.pallas_call(functools.partial(update_kernel, limit, step), out_shape=(...  5.3 us
    pallas_call x3, Pallas kernels, body(): pl.pallas_call(functools.partial(join_kernel, group, room, opens, ends),...  4.7 us
    pallas_call x1, Pallas kernels, body(): pl.pallas_call(functools.partial(pack_far_kernel, peers, rows_dev, room),...  4.6 us
    ppermute x3, starting transfers between devices, body(): got[hop] = lax.ppermute(packed_near[hop], 'dp', hop_pairs(hop, peers))  3.55 us
    pallas_call x1, Pallas kernels, body(): pl.pallas_call(functools.partial(pack_near_kernel, peers, rows_dev, room)...  2.26 us
  transfers between devices with their start and end apart: 7, of which 0 were waited for; matrix products, arithmetic and copies ran while one was open for 0% of the time, Pallas kernels for 14%

profile of v4, /device:TPU:0, one launch (start us, length us, event | category | flops | bytes accessed | tf_op | source)
XLA Modules:
  0.0 44.1 jit_solution(13020263563913255572)
XLA Ops:
  0.6 4.6 %pack_far.1 = (s16[272,128]{1,0:T(8,128)(2,1)S(1)}, s16[272,128]{1,0:T(8,128)(2,1)S(1)}, s16[272,128]{1,0:T(8,128)(2,1)S(1)}, s16[272,128]{1,0:T(8,128)(2,1)S(1)...) custom-call(s32[1,2048]{1,0:T(1,128)} %bitcast.1, ...), custom_call_target="tpu_custom_call" | custom-call | tf_op jit(solution)/shard_map/pack_far/pallas_call | solution.py:310
  5.2 5.0 %collective-permute-start.1 = (s16[272,128]{1,0:T(8,128)(2,1)S(1)}, s16[272,128]{1,0:T(8,128)(2,1)S(1)}, u32[]{:S(2)}, u32[]{:S(2)}) collective-permute-start(s16[272,128]{1,0:T(8,128)(2,1)S(1)} %get-tuple-element.24), channel_id=1, source_target_pairs={{0,20},{4,16},{8,28},{12,24},{16,4},{20,0},{24,12},{28,8},{1,21},{... | collective-permute-start | bytes 208904 | tf_op jit(solution)/shard_map/ppermute | solution.py:326
  10.3 1.3 %collective-permute-start.5 = (s16[272,128]{1,0:T(8,128)(2,1)S(1)}, s16[272,128]{1,0:T(8,128)(2,1)S(1)}, u32[]{:S(2)}, u32[]{:S(2)}) collective-permute-start(s16[272,128]{1,0:T(8,128)(2,1)S(1)} %get-tuple-element.32), channel_id=1, source_target_pairs={{0,28},{4,24},{8,20},{12,16},{16,12},{20,8},{24,4},{28,0},{1,29},{... | collective-permute-start | bytes 208904 | tf_op jit(solution)/shard_map/ppermute | solution.py:326
  11.6 2.5 %collective-permute-start.6 = (s16[272,128]{1,0:T(8,128)(2,1)S(1)}, s16[272,128]{1,0:T(8,128)(2,1)S(1)}, u32[]{:S(2)}, u32[]{:S(2)}) collective-permute-start(s16[272,128]{1,0:T(8,128)(2,1)S(1)} %get-tuple-element.33), channel_id=1, source_target_pairs={{0,24},{4,28},{8,16},{12,20},{16,8},{20,12},{24,0},{28,4},{1,25},{... | collective-permute-start | bytes 208904 | tf_op jit(solution)/shard_map/ppermute | solution.py:326
  14.0 2.3 %pack_near.1 = (s16[272,128]{1,0:T(8,128)(2,1)S(1)}, s16[272,128]{1,0:T(8,128)(2,1)S(1)}, s16[272,128]{1,0:T(8,128)(2,1)S(1)}, s16[272,128]{1,0:T(8,128)(2,1)S(1)}, f32[8192,128]{1,0:T(8,128)S(1)}) custom-call(s32[1,2048]{1,0:T(1,128)S(1)} %get-tuple-element.25.rel_ref, s32[1,2048]{1,0:T(1,128)S(1)} %get-tuple-element.26.rank_ref, ...), custom_call_target="tpu_custom_call" | custom-call | flops 1073741824 | bytes 16777216 | tf_op jit(solution)/shard_map/pack_near/pallas_call | solution.py:327
  16.3 0.8 %collective-permute-start.2 = (s16[272,128]{1,0:T(8,128)(2,1)S(1)}, s16[272,128]{1,0:T(8,128)(2,1)S(1)}, u32[]{:S(2)}, u32[]{:S(2)}) collective-permute-start(s16[272,128]{1,0:T(8,128)(2,1)S(1)} %get-tuple-element.28), channel_id=1, source_target_pairs={{0,12},{4,8},{8,4},{12,0},{16,28},{20,24},{24,20},{28,16},{1,13},{... | collective-permute-start | bytes 208904 | tf_op jit(solution)/shard_map/ppermute | solution.py:339
  17.1 2.3 %collective-permute-start.3 = (s16[272,128]{1,0:T(8,128)(2,1)S(1)}, s16[272,128]{1,0:T(8,128)(2,1)S(1)}, u32[]{:S(2)}, u32[]{:S(2)}) collective-permute-start(s16[272,128]{1,0:T(8,128)(2,1)S(1)} %get-tuple-element.29), channel_id=1, source_target_pairs={{0,8},{4,12},{8,0},{12,4},{16,24},{20,28},{24,16},{28,20},{1,9},{5... | collective-permute-start | bytes 208904 | tf_op jit(solution)/shard_map/ppermute | solution.py:339
  19.4 0.0 collective-permute-done.5.refs_1_
  19.4 0.5 %collective-permute-start.4 = (s16[272,128]{1,0:T(8,128)(2,1)S(1)}, s16[272,128]{1,0:T(8,128)(2,1)S(1)}, u32[]{:S(2)}, u32[]{:S(2)}) collective-permute-start(s16[272,128]{1,0:T(8,128)(2,1)S(1)} %get-tuple-element.30), channel_id=1, source_target_pairs={{0,4},{4,0},{8,12},{12,8},{16,20},{20,16},{24,28},{28,24},{1,5},{5... | collective-permute-start | bytes 208904 | tf_op jit(solution)/shard_map/ppermute | solution.py:339
  19.9 0.0 collective-permute-done.6.refs_2_
  19.9 3.4 %collective-permute-start = (s16[272,128]{1,0:T(8,128)(2,1)S(1)}, s16[272,128]{1,0:T(8,128)(2,1)S(1)}, u32[]{:S(2)}, u32[]{:S(2)}) collective-permute-start(s16[272,128]{1,0:T(8,128)(2,1)S(1)} %get-tuple-element.23), channel_id=1, source_target_pairs={{0,16},{4,20},{8,24},{12,28},{16,0},{20,4},{24,8},{28,12},{1,17},{... | collective-permute-start | bytes 208904 | tf_op jit(solution)/shard_map/ppermute | solution.py:326
  23.3 1.3 %join_rows_0.1 = (f32[8200,128]{1,0:T(8,128)S(1)}, f32[8,128]{1,0:T(8,128)S(1)}) custom-call(s16[272,128]{1,0:T(8,128)(2,1)S(1)} %get-tuple-element.31.refs_0_, s16[272,128]{1,0:T(8,128)(2,1)S(1)} %collective-permute-done.5.refs_1_, s16[272,128]{1,0:T(8,128)(2,1)S(1)} %collective-permute-done.6.refs_2_), custom_call_target="tpu_custom_call" | custom-call | flops 128 | bytes 128 | tf_op jit(solution)/shard_map/join_rows_0/pallas_call | solution.py:355
  24.6 0.0 collective-permute-done.1.refs_0_
  24.6 0.0 collective-permute-done.2.refs_1_
  24.6 0.0 collective-permute-done.3.refs_2_
  24.7 0.0 collective-permute-done.4.refs_3_
  24.7 2.4 %join_rows_1.1 = (f32[8200,128]{1,0:T(8,128)S(1)}, f32[8,128]{1,0:T(8,128)S(1)}, f32[8192,128]{1,0:T(8,128)S(1)}) custom-call(s16[272,128]{1,0:T(8,128)(2,1)S(1)} %collective-permute-done.1.refs_0_, s16[272,128]{1,0:T(8,128)(2,1)S(1)} %collective-permute-done.2.refs_1_, ...), custom_call_target="tpu_custom_call", output_to_operand_aliasing={{0}: (4, {})} | custom-call | flops 128 | bytes 128 | tf_op jit(solution)/shard_map/join_rows_1/pallas_call | solution.py:355
  27.0 0.0 collective-permute-done.refs_0_
  27.1 1.0 %join_rows_2.1 = (f32[8200,128]{1,0:T(8,128)S(1)}, f32[32,1,128]{2,1,0:T(1,128)S(1)}) custom-call(s16[272,128]{1,0:T(8,128)(2,1)S(1)} %collective-permute-done.refs_0_, f32[8200,128]{1,0:T(8,128)S(1)} %get-tuple-element.36.refs_1_, f32[8,128]{1,0:T(8,128)S(1)} %get-tuple-element.37.refs_2_), custom_call_target="tpu_custom_call", output_to_operand_aliasing={{0}: (1, {})} | custom-call | flops 128 | bytes 128 | tf_op jit(solution)/shard_map/join_rows_2/pallas_call | solution.py:355
  28.1 10.6 %all_to_all.5.parts_ref = f32[32,1,128]{2,1,0:T(1,128)S(1)} all-to-all(f32[32,1,128]{2,1,0:T(1,128)S(1)} %get-tuple-element.38), channel_id=1, replica_groups=mesh['dp'=8,'mp'=4] {'dp','mp'}, dimensions={0} | all-to-all | bytes 32768 | tf_op jit(solution)/shard_map/all_to_all | solution.py:376
  38.7 5.3 %update_rows.1 = (f32[8192,128]{1,0:T(8,128)}, f32[8192,128]{1,0:T(8,128)}, f32[8192,128]{1,0:T(8,128)}) custom-call(f32[32,1,128]{2,1,0:T(1,128)S(1)} %all_to_all.5.parts_ref, f32[8200,128]{1,0:T(8,128)S(1)} %get-tuple-element.39.grad_ref, f32[8192,128]{1,0:T(8,128)S(1)} %get-tuple-element.40.table_ref, f32[8192,128]{1,0:T(8,128)S(1)} %get-tuple-element.41.first_ref, ...), custom_call_target="tpu_custom_call" | custom-call | tf_op jit(solution)/shard_map/update_rows/pallas_call | solution.py:379
Async XLA Ops:
  5.2 19.4 %collective-permute-start.1 = (s16[272,128]{1,0:T(8,128)(2,1)S(1)}, s16[272,128]{1,0:T(8,128)(2,1)S(1)}, u32[]{:S(2)}, u32[]{:S(2)}) collective-permute-start(s16[272,128]{1,0:T(8,128)(2,1)S(1)} %get-tuple-element.24), channel_id=1, source_target_pairs={{0,20},{4,16},{8,28},{12,24},{16,4},{20,0},{24,12},{28,8},{1,21},{... | collective-permute-start | bytes 208904 | tf_op jit(solution)/shard_map/ppermute | solution.py:326
  10.3 9.1 %collective-permute-start.5 = (s16[272,128]{1,0:T(8,128)(2,1)S(1)}, s16[272,128]{1,0:T(8,128)(2,1)S(1)}, u32[]{:S(2)}, u32[]{:S(2)}) collective-permute-start(s16[272,128]{1,0:T(8,128)(2,1)S(1)} %get-tuple-element.32), channel_id=1, source_target_pairs={{0,28},{4,24},{8,20},{12,16},{16,12},{20,8},{24,4},{28,0},{1,29},{... | collective-permute-start | bytes 208904 | tf_op jit(solution)/shard_map/ppermute | solution.py:326
  11.6 8.3 %collective-permute-start.6 = (s16[272,128]{1,0:T(8,128)(2,1)S(1)}, s16[272,128]{1,0:T(8,128)(2,1)S(1)}, u32[]{:S(2)}, u32[]{:S(2)}) collective-permute-start(s16[272,128]{1,0:T(8,128)(2,1)S(1)} %get-tuple-element.33), channel_id=1, source_target_pairs={{0,24},{4,28},{8,16},{12,20},{16,8},{20,12},{24,0},{28,4},{1,25},{... | collective-permute-start | bytes 208904 | tf_op jit(solution)/shard_map/ppermute | solution.py:326
  16.3 8.3 %collective-permute-start.2 = (s16[272,128]{1,0:T(8,128)(2,1)S(1)}, s16[272,128]{1,0:T(8,128)(2,1)S(1)}, u32[]{:S(2)}, u32[]{:S(2)}) collective-permute-start(s16[272,128]{1,0:T(8,128)(2,1)S(1)} %get-tuple-element.28), channel_id=1, source_target_pairs={{0,12},{4,8},{8,4},{12,0},{16,28},{20,24},{24,20},{28,16},{1,13},{... | collective-permute-start | bytes 208904 | tf_op jit(solution)/shard_map/ppermute | solution.py:339
  17.1 7.5 %collective-permute-start.3 = (s16[272,128]{1,0:T(8,128)(2,1)S(1)}, s16[272,128]{1,0:T(8,128)(2,1)S(1)}, u32[]{:S(2)}, u32[]{:S(2)}) collective-permute-start(s16[272,128]{1,0:T(8,128)(2,1)S(1)} %get-tuple-element.29), channel_id=1, source_target_pairs={{0,8},{4,12},{8,0},{12,4},{16,24},{20,28},{24,16},{28,20},{1,9},{5... | collective-permute-start | bytes 208904 | tf_op jit(solution)/shard_map/ppermute | solution.py:339
  19.4 5.3 %collective-permute-start.4 = (s16[272,128]{1,0:T(8,128)(2,1)S(1)}, s16[272,128]{1,0:T(8,128)(2,1)S(1)}, u32[]{:S(2)}, u32[]{:S(2)}) collective-permute-start(s16[272,128]{1,0:T(8,128)(2,1)S(1)} %get-tuple-element.30), channel_id=1, source_target_pairs={{0,4},{4,0},{8,12},{12,8},{16,20},{20,16},{24,28},{28,24},{1,5},{5... | collective-permute-start | bytes 208904 | tf_op jit(solution)/shard_map/ppermute | solution.py:339
  19.9 7.2 %collective-permute-start = (s16[272,128]{1,0:T(8,128)(2,1)S(1)}, s16[272,128]{1,0:T(8,128)(2,1)S(1)}, u32[]{:S(2)}, u32[]{:S(2)}) collective-permute-start(s16[272,128]{1,0:T(8,128)(2,1)S(1)} %get-tuple-element.23), channel_id=1, source_target_pairs={{0,16},{4,20},{8,24},{12,28},{16,0},{20,4},{24,8},{28,12},{1,17},{... | collective-permute-start | bytes 208904 | tf_op jit(solution)/shard_map/ppermute | solution.py:326

commit v5 on v4

--- a/solution.py
+++ b/solution.py
@@ -277,7 +277,8 @@
         first_buf[part, :] = new_first
         new_second = beta_second * second_ref[part, :] + (1.0 - beta_second) * clipped * clipped
         second_buf[part, :] = new_second
-        change = (new_first * (learn_rate / first_fix)) / (jnp.sqrt(new_second * (1.0 / second_fix)) + adam_eps)
+        spread = new_second * (1.0 / second_fix)
+        change = (new_first * (learn_rate / first_fix)) / (spread * lax.rsqrt(spread) + adam_eps)
         table_buf[part, :] = table_ref[part, :] * (1.0 - learn_rate * decay_rate) - change
         for k, (a, b) in enumerate(((first_buf, first_out), (second_buf, second_out), (table_buf, table_out))):
             copy = pltpu.make_async_copy(a.at[part], b.at[part], sems.at[k, n])
@@ -340,7 +341,7 @@
     longer = pltpu.VMEM((rows_dev + 8, width), f32)
 
     half, most = far // 2, 3 * far // 4
-    hops = list(range(peers - 1, 0, -1))
+    hops = [*range(near + far // 2, peers), *range(near + far // 2 - 1, 0, -1)]
     rounds = [[0, *hops[:half]], [*hops[half:most], *hops[far:]], hops[most:far]]
     grad_rows = part = None
     for n, members in enumerate(rounds):

time: 44.4 us -> 43.3 us (0.975)
  no operation moved by 1% of the time
where the time goes in v5:
time: 43.3 us; the launch traced here: 43 us
  Pallas kernels  16.5 us (38%)
  starting transfers between devices  15.4 us (36%)
  blocking collectives  10.2 us (24%)
  between operations  0.88 us (2%)
    ppermute x4, starting transfers between devices, body(): got[hop] = lax.ppermute(packed_far[hop - near], 'dp', hop_pairs(hop, peers))  11.9 us
    all_to_all x1, blocking collectives, body(): lax.all_to_all(part, ('dp', 'mp'), split_axis=0, concat_axis=0, tiled=True)  10.2 us
    pallas_call x1, Pallas kernels, body(): pl.pallas_call(functools.partial(update_kernel, limit, step), out_shape=(...  4.91 us
    pallas_call x3, Pallas kernels, body(): pl.pallas_call(functools.partial(join_kernel, group, room, opens, ends),...  4.7 us
    pallas_call x1, Pallas kernels, body(): pl.pallas_call(functools.partial(pack_far_kernel, peers, rows_dev, room),...  4.6 us
    ppermute x3, starting transfers between devices, body(): got[hop] = lax.ppermute(packed_near[hop], 'dp', hop_pairs(hop, peers))  3.55 us
    pallas_call x1, Pallas kernels, body(): pl.pallas_call(functools.partial(pack_near_kernel, peers, rows_dev, room)...  2.26 us
  transfers between devices with their start and end apart: 7, of which 0 were waited for; matrix products, arithmetic and copies ran while one was open for 0% of the time, Pallas kernels for 14%

profile of v5, /device:TPU:0, one launch (start us, length us, event | category | flops | bytes accessed | tf_op | source)
XLA Modules:
  0.0 43.0 jit_solution(10034948054351675753)
XLA Ops:
  0.6 4.6 %pack_far.1 = (s16[272,128]{1,0:T(8,128)(2,1)S(1)}, s16[272,128]{1,0:T(8,128)(2,1)S(1)}, s16[272,128]{1,0:T(8,128)(2,1)S(1)}, s16[272,128]{1,0:T(8,128)(2,1)S(1)...) custom-call(s32[1,2048]{1,0:T(1,128)} %bitcast.1, ...), custom_call_target="tpu_custom_call" | custom-call | tf_op jit(solution)/shard_map/pack_far/pallas_call | solution.py:311
  5.2 5.0 %collective-permute-start.1 = (s16[272,128]{1,0:T(8,128)(2,1)S(1)}, s16[272,128]{1,0:T(8,128)(2,1)S(1)}, u32[]{:S(2)}, u32[]{:S(2)}) collective-permute-start(s16[272,128]{1,0:T(8,128)(2,1)S(1)} %get-tuple-element.24), channel_id=1, source_target_pairs={{0,20},{4,16},{8,28},{12,24},{16,4},{20,0},{24,12},{28,8},{1,21},{... | collective-permute-start | bytes 208904 | tf_op jit(solution)/shard_map/ppermute | solution.py:327
  10.3 1.4 %collective-permute-start.5 = (s16[272,128]{1,0:T(8,128)(2,1)S(1)}, s16[272,128]{1,0:T(8,128)(2,1)S(1)}, u32[]{:S(2)}, u32[]{:S(2)}) collective-permute-start(s16[272,128]{1,0:T(8,128)(2,1)S(1)} %get-tuple-element.32), channel_id=1, source_target_pairs={{0,24},{4,28},{8,16},{12,20},{16,8},{20,12},{24,0},{28,4},{1,25},{... | collective-permute-start | bytes 208904 | tf_op jit(solution)/shard_map/ppermute | solution.py:327
  11.6 2.4 %collective-permute-start.6 = (s16[272,128]{1,0:T(8,128)(2,1)S(1)}, s16[272,128]{1,0:T(8,128)(2,1)S(1)}, u32[]{:S(2)}, u32[]{:S(2)}) collective-permute-start(s16[272,128]{1,0:T(8,128)(2,1)S(1)} %get-tuple-element.33), channel_id=1, source_target_pairs={{0,28},{4,24},{8,20},{12,16},{16,12},{20,8},{24,4},{28,0},{1,29},{... | collective-permute-start | bytes 208904 | tf_op jit(solution)/shard_map/ppermute | solution.py:327
  14.0 2.3 %pack_near.1 = (s16[272,128]{1,0:T(8,128)(2,1)S(1)}, s16[272,128]{1,0:T(8,128)(2,1)S(1)}, s16[272,128]{1,0:T(8,128)(2,1)S(1)}, s16[272,128]{1,0:T(8,128)(2,1)S(1)}, f32[8192,128]{1,0:T(8,128)S(1)}) custom-call(s32[1,2048]{1,0:T(1,128)S(1)} %get-tuple-element.25.rel_ref, s32[1,2048]{1,0:T(1,128)S(1)} %get-tuple-element.26.rank_ref, ...), custom_call_target="tpu_custom_call" | custom-call | flops 1073741824 | bytes 16777216 | tf_op jit(solution)/shard_map/pack_near/pallas_call | solution.py:328
  16.3 0.8 %collective-permute-start.2 = (s16[272,128]{1,0:T(8,128)(2,1)S(1)}, s16[272,128]{1,0:T(8,128)(2,1)S(1)}, u32[]{:S(2)}, u32[]{:S(2)}) collective-permute-start(s16[272,128]{1,0:T(8,128)(2,1)S(1)} %get-tuple-element.28), channel_id=1, source_target_pairs={{0,12},{4,8},{8,4},{12,0},{16,28},{20,24},{24,20},{28,16},{1,13},{... | collective-permute-start | bytes 208904 | tf_op jit(solution)/shard_map/ppermute | solution.py:340
  17.1 2.3 %collective-permute-start.3 = (s16[272,128]{1,0:T(8,128)(2,1)S(1)}, s16[272,128]{1,0:T(8,128)(2,1)S(1)}, u32[]{:S(2)}, u32[]{:S(2)}) collective-permute-start(s16[272,128]{1,0:T(8,128)(2,1)S(1)} %get-tuple-element.29), channel_id=1, source_target_pairs={{0,8},{4,12},{8,0},{12,4},{16,24},{20,28},{24,16},{28,20},{1,9},{5... | collective-permute-start | bytes 208904 | tf_op jit(solution)/shard_map/ppermute | solution.py:340
  19.4 0.0 collective-permute-done.5.refs_1_
  19.4 0.5 %collective-permute-start.4 = (s16[272,128]{1,0:T(8,128)(2,1)S(1)}, s16[272,128]{1,0:T(8,128)(2,1)S(1)}, u32[]{:S(2)}, u32[]{:S(2)}) collective-permute-start(s16[272,128]{1,0:T(8,128)(2,1)S(1)} %get-tuple-element.30), channel_id=1, source_target_pairs={{0,4},{4,0},{8,12},{12,8},{16,20},{20,16},{24,28},{28,24},{1,5},{5... | collective-permute-start | bytes 208904 | tf_op jit(solution)/shard_map/ppermute | solution.py:340
  19.9 0.0 collective-permute-done.6.refs_2_
  19.9 3.1 %collective-permute-start = (s16[272,128]{1,0:T(8,128)(2,1)S(1)}, s16[272,128]{1,0:T(8,128)(2,1)S(1)}, u32[]{:S(2)}, u32[]{:S(2)}) collective-permute-start(s16[272,128]{1,0:T(8,128)(2,1)S(1)} %get-tuple-element.23), channel_id=1, source_target_pairs={{0,16},{4,20},{8,24},{12,28},{16,0},{20,4},{24,8},{28,12},{1,17},{... | collective-permute-start | bytes 208904 | tf_op jit(solution)/shard_map/ppermute | solution.py:327
  22.9 1.3 %join_rows_0.1 = (f32[8200,128]{1,0:T(8,128)S(1)}, f32[8,128]{1,0:T(8,128)S(1)}) custom-call(s16[272,128]{1,0:T(8,128)(2,1)S(1)} %get-tuple-element.31.refs_0_, s16[272,128]{1,0:T(8,128)(2,1)S(1)} %collective-permute-done.5.refs_1_, s16[272,128]{1,0:T(8,128)(2,1)S(1)} %collective-permute-done.6.refs_2_), custom_call_target="tpu_custom_call" | custom-call | flops 128 | bytes 128 | tf_op jit(solution)/shard_map/join_rows_0/pallas_call | solution.py:356
  24.3 0.0 collective-permute-done.1.refs_0_
  24.3 0.0 collective-permute-done.2.refs_1_
  24.3 0.0 collective-permute-done.3.refs_2_
  24.3 0.0 collective-permute-done.4.refs_3_
  24.3 2.4 %join_rows_1.1 = (f32[8200,128]{1,0:T(8,128)S(1)}, f32[8,128]{1,0:T(8,128)S(1)}, f32[8192,128]{1,0:T(8,128)S(1)}) custom-call(s16[272,128]{1,0:T(8,128)(2,1)S(1)} %collective-permute-done.1.refs_0_, s16[272,128]{1,0:T(8,128)(2,1)S(1)} %collective-permute-done.2.refs_1_, ...), custom_call_target="tpu_custom_call", output_to_operand_aliasing={{0}: (4, {})} | custom-call | flops 128 | bytes 128 | tf_op jit(solution)/shard_map/join_rows_1/pallas_call | solution.py:356
  26.7 0.0 collective-permute-done.refs_0_
  26.7 1.0 %join_rows_2.1 = (f32[8200,128]{1,0:T(8,128)S(1)}, f32[32,1,128]{2,1,0:T(1,128)S(1)}) custom-call(s16[272,128]{1,0:T(8,128)(2,1)S(1)} %collective-permute-done.refs_0_, f32[8200,128]{1,0:T(8,128)S(1)} %get-tuple-element.36.refs_1_, f32[8,128]{1,0:T(8,128)S(1)} %get-tuple-element.37.refs_2_), custom_call_target="tpu_custom_call", output_to_operand_aliasing={{0}: (1, {})} | custom-call | flops 128 | bytes 128 | tf_op jit(solution)/shard_map/join_rows_2/pallas_call | solution.py:356
  27.7 10.2 %all_to_all.5.parts_ref = f32[32,1,128]{2,1,0:T(1,128)S(1)} all-to-all(f32[32,1,128]{2,1,0:T(1,128)S(1)} %get-tuple-element.38), channel_id=1, replica_groups=mesh['dp'=8,'mp'=4] {'dp','mp'}, dimensions={0} | all-to-all | bytes 32768 | tf_op jit(solution)/shard_map/all_to_all | solution.py:377
  38.0 4.9 %update_rows.1 = (f32[8192,128]{1,0:T(8,128)}, f32[8192,128]{1,0:T(8,128)}, f32[8192,128]{1,0:T(8,128)}) custom-call(f32[32,1,128]{2,1,0:T(1,128)S(1)} %all_to_all.5.parts_ref, f32[8200,128]{1,0:T(8,128)S(1)} %get-tuple-element.39.grad_ref, f32[8192,128]{1,0:T(8,128)S(1)} %get-tuple-element.40.table_ref, f32[8192,128]{1,0:T(8,128)S(1)} %get-tuple-element.41.first_ref, ...), custom_call_target="tpu_custom_call" | custom-call | tf_op jit(solution)/shard_map/update_rows/pallas_call | solution.py:380
Async XLA Ops:
  5.2 19.1 %collective-permute-start.1 = (s16[272,128]{1,0:T(8,128)(2,1)S(1)}, s16[272,128]{1,0:T(8,128)(2,1)S(1)}, u32[]{:S(2)}, u32[]{:S(2)}) collective-permute-start(s16[272,128]{1,0:T(8,128)(2,1)S(1)} %get-tuple-element.24), channel_id=1, source_target_pairs={{0,20},{4,16},{8,28},{12,24},{16,4},{20,0},{24,12},{28,8},{1,21},{... | collective-permute-start | bytes 208904 | tf_op jit(solution)/shard_map/ppermute | solution.py:327
  10.3 9.1 %collective-permute-start.5 = (s16[272,128]{1,0:T(8,128)(2,1)S(1)}, s16[272,128]{1,0:T(8,128)(2,1)S(1)}, u32[]{:S(2)}, u32[]{:S(2)}) collective-permute-start(s16[272,128]{1,0:T(8,128)(2,1)S(1)} %get-tuple-element.32), channel_id=1, source_target_pairs={{0,24},{4,28},{8,16},{12,20},{16,8},{20,12},{24,0},{28,4},{1,25},{... | collective-permute-start | bytes 208904 | tf_op jit(solution)/shard_map/ppermute | solution.py:327
  11.6 8.2 %collective-permute-start.6 = (s16[272,128]{1,0:T(8,128)(2,1)S(1)}, s16[272,128]{1,0:T(8,128)(2,1)S(1)}, u32[]{:S(2)}, u32[]{:S(2)}) collective-permute-start(s16[272,128]{1,0:T(8,128)(2,1)S(1)} %get-tuple-element.33), channel_id=1, source_target_pairs={{0,28},{4,24},{8,20},{12,16},{16,12},{20,8},{24,4},{28,0},{1,29},{... | collective-permute-start | bytes 208904 | tf_op jit(solution)/shard_map/ppermute | solution.py:327
  16.3 8.0 %collective-permute-start.2 = (s16[272,128]{1,0:T(8,128)(2,1)S(1)}, s16[272,128]{1,0:T(8,128)(2,1)S(1)}, u32[]{:S(2)}, u32[]{:S(2)}) collective-permute-start(s16[272,128]{1,0:T(8,128)(2,1)S(1)} %get-tuple-element.28), channel_id=1, source_target_pairs={{0,12},{4,8},{8,4},{12,0},{16,28},{20,24},{24,20},{28,16},{1,13},{... | collective-permute-start | bytes 208904 | tf_op jit(solution)/shard_map/ppermute | solution.py:340
  17.1 7.2 %collective-permute-start.3 = (s16[272,128]{1,0:T(8,128)(2,1)S(1)}, s16[272,128]{1,0:T(8,128)(2,1)S(1)}, u32[]{:S(2)}, u32[]{:S(2)}) collective-permute-start(s16[272,128]{1,0:T(8,128)(2,1)S(1)} %get-tuple-element.29), channel_id=1, source_target_pairs={{0,8},{4,12},{8,0},{12,4},{16,24},{20,28},{24,16},{28,20},{1,9},{5... | collective-permute-start | bytes 208904 | tf_op jit(solution)/shard_map/ppermute | solution.py:340
  19.4 5.0 %collective-permute-start.4 = (s16[272,128]{1,0:T(8,128)(2,1)S(1)}, s16[272,128]{1,0:T(8,128)(2,1)S(1)}, u32[]{:S(2)}, u32[]{:S(2)}) collective-permute-start(s16[272,128]{1,0:T(8,128)(2,1)S(1)} %get-tuple-element.30), channel_id=1, source_target_pairs={{0,4},{4,0},{8,12},{12,8},{16,20},{20,16},{24,28},{28,24},{1,5},{5... | collective-permute-start | bytes 208904 | tf_op jit(solution)/shard_map/ppermute | solution.py:340
  19.9 6.8 %collective-permute-start = (s16[272,128]{1,0:T(8,128)(2,1)S(1)}, s16[272,128]{1,0:T(8,128)(2,1)S(1)}, u32[]{:S(2)}, u32[]{:S(2)}) collective-permute-start(s16[272,128]{1,0:T(8,128)(2,1)S(1)} %get-tuple-element.23), channel_id=1, source_target_pairs={{0,16},{4,20},{8,24},{12,28},{16,0},{20,4},{24,8},{28,12},{1,17},{... | collective-permute-start | bytes 208904 | tf_op jit(solution)/shard_map/ppermute | solution.py:327

commit v6 on v5

--- a/solution.py
+++ b/solution.py
@@ -214,11 +214,10 @@
     return [range(k, min(k + per_block, lines)) for k in range(0, lines, per_block)]
 
 
-def join_kernel(group, room, opens, ends, *refs):
+def join_kernel(group, room, opens, ends, middle, *refs):
     got, refs = refs[:group], refs[group:]
     if not opens:
         (_, sum_ref), refs = refs[:2], refs[2:]
-    middle = not opens and not ends
     if middle:
         state_hbm, grad_ref, part_ref, state_ref, *refs, state_sem = refs
         state_copy = pltpu.make_async_copy(state_hbm, state_ref, state_sem)
@@ -340,13 +339,13 @@
         got[hop] = lax.ppermute(packed_near[hop], "dp", hop_pairs(hop, peers))
     longer = pltpu.VMEM((rows_dev + 8, width), f32)
 
-    half, most = far // 2, 3 * far // 4
+    lead, half, most = far // 4, far // 2, 3 * far // 4
     hops = [*range(near + far // 2, peers), *range(near + far // 2 - 1, 0, -1)]
-    rounds = [[0, *hops[:half]], [*hops[half:most], *hops[far:]], hops[most:far]]
+    rounds = [[0, *hops[:lead]], [*hops[lead:most], *hops[far:]], hops[most:far]]
     grad_rows = part = None
     for n, members in enumerate(rounds):
         opens, ends = n == 0, n == len(rounds) - 1
-        middle = not opens and not ends
+        middle = n == 1
         group = len(members)
         operands = [got[hop] for hop in members]
         if not opens:
@@ -354,7 +353,7 @@
         if middle:
             operands.append(in_hbm(first_moment))
         grad_rows, part, *state = pl.pallas_call(
-            functools.partial(join_kernel, group, room, opens, ends),
+            functools.partial(join_kernel, group, room, opens, ends, middle),
             out_shape=(longer, shape((everyone, 1, width) if ends else (8, LANES), f32)) + (kept,) * middle,
             in_specs=[vmem] * (len(operands) - middle) + [hbm] * middle,
             out_specs=(vmem,) * (2 + middle),

time: 43.3 us -> 42.5 us (0.982)
  starting transfers between devices: 15.4 us -> 14.5 us
    ppermute x4, starting transfers between devices: 11.9 us -> 10.9 us  [body(): got[hop] = lax.ppermute(packed_far[hop - near], 'dp', hop_pairs(hop, peers))]
where the time goes in v6:
time: 42.5 us; the launch traced here: 42.3 us
  Pallas kernels  16.5 us (39%)
  starting transfers between devices  14.5 us (34%)
  blocking collectives  10.4 us (24%)
  between operations  0.88 us (2%)
    ppermute x4, starting transfers between devices, body(): got[hop] = lax.ppermute(packed_far[hop - near], 'dp', hop_pairs(hop, peers))  10.9 us
    all_to_all x1, blocking collectives, body(): lax.all_to_all(part, ('dp', 'mp'), split_axis=0, concat_axis=0, tiled=True)  10.4 us
    pallas_call x1, Pallas kernels, body(): pl.pallas_call(functools.partial(update_kernel, limit, step), out_shape=(...  4.9 us
    pallas_call x3, Pallas kernels, body(): pl.pallas_call(functools.partial(join_kernel, group, room, opens, ends, m...  4.74 us
    pallas_call x1, Pallas kernels, body(): pl.pallas_call(functools.partial(pack_far_kernel, peers, rows_dev, room),...  4.6 us
    ppermute x3, starting transfers between devices, body(): got[hop] = lax.ppermute(packed_near[hop], 'dp', hop_pairs(hop, peers))  3.55 us
    pallas_call x1, Pallas kernels, body(): pl.pallas_call(functools.partial(pack_near_kernel, peers, rows_dev, room)...  2.26 us
  transfers between devices with their start and end apart: 7, of which 0 were waited for; matrix products, arithmetic and copies ran while one was open for 0% of the time, Pallas kernels for 14%

profile of v6, /device:TPU:0, one launch (start us, length us, event | category | flops | bytes accessed | tf_op | source)
XLA Modules:
  0.0 42.3 jit_solution(916941236652270118)
XLA Ops:
  0.6 4.6 %pack_far.1 = (s16[272,128]{1,0:T(8,128)(2,1)S(1)}, s16[272,128]{1,0:T(8,128)(2,1)S(1)}, s16[272,128]{1,0:T(8,128)(2,1)S(1)}, s16[272,128]{1,0:T(8,128)(2,1)S(1)...) custom-call(s32[1,2048]{1,0:T(1,128)} %bitcast.1, ...), custom_call_target="tpu_custom_call" | custom-call | tf_op jit(solution)/shard_map/pack_far/pallas_call | solution.py:310
  5.2 6.0 %collective-permute-start.1 = (s16[272,128]{1,0:T(8,128)(2,1)S(1)}, s16[272,128]{1,0:T(8,128)(2,1)S(1)}, u32[]{:S(2)}, u32[]{:S(2)}) collective-permute-start(s16[272,128]{1,0:T(8,128)(2,1)S(1)} %get-tuple-element.24), channel_id=1, source_target_pairs={{0,28},{4,24},{8,20},{12,16},{16,12},{20,8},{24,4},{28,0},{1,29},{... | collective-permute-start | bytes 208904 | tf_op jit(solution)/shard_map/ppermute | solution.py:326
  11.3 0.0 collective-permute-start.2
  11.3 1.9 %collective-permute-start.6 = (s16[272,128]{1,0:T(8,128)(2,1)S(1)}, s16[272,128]{1,0:T(8,128)(2,1)S(1)}, u32[]{:S(2)}, u32[]{:S(2)}) collective-permute-start(s16[272,128]{1,0:T(8,128)(2,1)S(1)} %get-tuple-element.33), channel_id=1, source_target_pairs={{0,24},{4,28},{8,16},{12,20},{16,8},{20,12},{24,0},{28,4},{1,25},{... | collective-permute-start | bytes 208904 | tf_op jit(solution)/shard_map/ppermute | solution.py:326
  13.1 2.3 %pack_near.1 = (s16[272,128]{1,0:T(8,128)(2,1)S(1)}, s16[272,128]{1,0:T(8,128)(2,1)S(1)}, s16[272,128]{1,0:T(8,128)(2,1)S(1)}, s16[272,128]{1,0:T(8,128)(2,1)S(1)}, f32[8192,128]{1,0:T(8,128)S(1)}) custom-call(s32[1,2048]{1,0:T(1,128)S(1)} %get-tuple-element.26.rel_ref, s32[1,2048]{1,0:T(1,128)S(1)} %get-tuple-element.27.rank_ref, ...), custom_call_target="tpu_custom_call" | custom-call | flops 1073741824 | bytes 16777216 | tf_op jit(solution)/shard_map/pack_near/pallas_call | solution.py:327
  15.4 2.6 %collective-permute-start.3 = (s16[272,128]{1,0:T(8,128)(2,1)S(1)}, s16[272,128]{1,0:T(8,128)(2,1)S(1)}, u32[]{:S(2)}, u32[]{:S(2)}) collective-permute-start(s16[272,128]{1,0:T(8,128)(2,1)S(1)} %get-tuple-element.29), channel_id=1, source_target_pairs={{0,12},{4,8},{8,4},{12,0},{16,28},{20,24},{24,20},{28,16},{1,13},{... | collective-permute-start | bytes 208904 | tf_op jit(solution)/shard_map/ppermute | solution.py:339
  18.0 0.5 %collective-permute-start.4 = (s16[272,128]{1,0:T(8,128)(2,1)S(1)}, s16[272,128]{1,0:T(8,128)(2,1)S(1)}, u32[]{:S(2)}, u32[]{:S(2)}) collective-permute-start(s16[272,128]{1,0:T(8,128)(2,1)S(1)} %get-tuple-element.30), channel_id=1, source_target_pairs={{0,8},{4,12},{8,0},{12,4},{16,24},{20,28},{24,16},{28,20},{1,9},{5... | collective-permute-start | bytes 208904 | tf_op jit(solution)/shard_map/ppermute | solution.py:339
  18.5 0.0 collective-permute-done.1.refs_0_
  18.5 0.5 %collective-permute-start.5 = (s16[272,128]{1,0:T(8,128)(2,1)S(1)}, s16[272,128]{1,0:T(8,128)(2,1)S(1)}, u32[]{:S(2)}, u32[]{:S(2)}) collective-permute-start(s16[272,128]{1,0:T(8,128)(2,1)S(1)} %get-tuple-element.31), channel_id=1, source_target_pairs={{0,4},{4,0},{8,12},{12,8},{16,20},{20,16},{24,28},{28,24},{1,5},{5... | collective-permute-start | bytes 208904 | tf_op jit(solution)/shard_map/ppermute | solution.py:339
  19.0 0.0 collective-permute-done.6.refs_1_
  19.0 3.0 %collective-permute-start = (s16[272,128]{1,0:T(8,128)(2,1)S(1)}, s16[272,128]{1,0:T(8,128)(2,1)S(1)}, u32[]{:S(2)}, u32[]{:S(2)}) collective-permute-start(s16[272,128]{1,0:T(8,128)(2,1)S(1)} %get-tuple-element.23), channel_id=1, source_target_pairs={{0,16},{4,20},{8,24},{12,28},{16,0},{20,4},{24,8},{28,12},{1,17},{... | collective-permute-start | bytes 208904 | tf_op jit(solution)/shard_map/ppermute | solution.py:326
  22.0 1.1 %join_rows_0.1 = (f32[8200,128]{1,0:T(8,128)S(1)}, f32[8,128]{1,0:T(8,128)S(1)}) custom-call(s16[272,128]{1,0:T(8,128)(2,1)S(1)} %get-tuple-element.32.refs_0_, s16[272,128]{1,0:T(8,128)(2,1)S(1)} %collective-permute-done.6.refs_1_), custom_call_target="tpu_custom_call" | custom-call | flops 128 | bytes 128 | tf_op jit(solution)/shard_map/join_rows_0/pallas_call | solution.py:355
  23.1 0.0 collective-permute-done.2.refs_1_
  23.1 0.0 collective-permute-done.3.refs_2_
  23.1 0.0 collective-permute-done.4.refs_3_
  23.1 0.0 collective-permute-done.5.refs_4_
  23.1 2.7 %join_rows_1.1 = (f32[8200,128]{1,0:T(8,128)S(1)}, f32[8,128]{1,0:T(8,128)S(1)}, f32[8192,128]{1,0:T(8,128)S(1)}) custom-call(s16[272,128]{1,0:T(8,128)(2,1)S(1)} %collective-permute-done.1.refs_0_, s16[272,128]{1,0:T(8,128)(2,1)S(1)} %collective-permute-done.2.refs_1_, ...), custom_call_target="tpu_custom_call", output_to_operand_aliasing={{0}: (5, {})} | custom-call | flops 128 | bytes 128 | tf_op jit(solution)/shard_map/join_rows_1/pallas_call | solution.py:355
  25.8 0.0 collective-permute-done.refs_0_
  25.8 1.0 %join_rows_2.1 = (f32[8200,128]{1,0:T(8,128)S(1)}, f32[32,1,128]{2,1,0:T(1,128)S(1)}) custom-call(s16[272,128]{1,0:T(8,128)(2,1)S(1)} %collective-permute-done.refs_0_, f32[8200,128]{1,0:T(8,128)S(1)} %get-tuple-element.36.refs_1_, f32[8,128]{1,0:T(8,128)S(1)} %get-tuple-element.37.refs_2_), custom_call_target="tpu_custom_call", output_to_operand_aliasing={{0}: (1, {})} | custom-call | flops 128 | bytes 128 | tf_op jit(solution)/shard_map/join_rows_2/pallas_call | solution.py:355
  26.8 10.4 %all_to_all.5.parts_ref = f32[32,1,128]{2,1,0:T(1,128)S(1)} all-to-all(f32[32,1,128]{2,1,0:T(1,128)S(1)} %get-tuple-element.38), channel_id=1, replica_groups=mesh['dp'=8,'mp'=4] {'dp','mp'}, dimensions={0} | all-to-all | bytes 32768 | tf_op jit(solution)/shard_map/all_to_all | solution.py:376
  37.2 4.9 %update_rows.1 = (f32[8192,128]{1,0:T(8,128)}, f32[8192,128]{1,0:T(8,128)}, f32[8192,128]{1,0:T(8,128)}) custom-call(f32[32,1,128]{2,1,0:T(1,128)S(1)} %all_to_all.5.parts_ref, f32[8200,128]{1,0:T(8,128)S(1)} %get-tuple-element.39.grad_ref, f32[8192,128]{1,0:T(8,128)S(1)} %get-tuple-element.40.table_ref, f32[8192,128]{1,0:T(8,128)S(1)} %get-tuple-element.41.first_ref, ...), custom_call_target="tpu_custom_call" | custom-call | tf_op jit(solution)/shard_map/update_rows/pallas_call | solution.py:379
Async XLA Ops:
  5.2 13.2 %collective-permute-start.1 = (s16[272,128]{1,0:T(8,128)(2,1)S(1)}, s16[272,128]{1,0:T(8,128)(2,1)S(1)}, u32[]{:S(2)}, u32[]{:S(2)}) collective-permute-start(s16[272,128]{1,0:T(8,128)(2,1)S(1)} %get-tuple-element.24), channel_id=1, source_target_pairs={{0,28},{4,24},{8,20},{12,16},{16,12},{20,8},{24,4},{28,0},{1,29},{... | collective-permute-start | bytes 208904 | tf_op jit(solution)/shard_map/ppermute | solution.py:326
  11.3 11.8 %collective-permute-start.2 = (s16[272,128]{1,0:T(8,128)(2,1)S(1)}, s16[272,128]{1,0:T(8,128)(2,1)S(1)}, u32[]{:S(2)}, u32[]{:S(2)}) collective-permute-start(s16[272,128]{1,0:T(8,128)(2,1)S(1)} %get-tuple-element.25), channel_id=1, source_target_pairs={{0,20},{4,16},{8,28},{12,24},{16,4},{20,0},{24,12},{28,8},{1,21},{... | collective-permute-start | bytes 208904 | tf_op jit(solution)/shard_map/ppermute | solution.py:326
  11.3 7.7 %collective-permute-start.6 = (s16[272,128]{1,0:T(8,128)(2,1)S(1)}, s16[272,128]{1,0:T(8,128)(2,1)S(1)}, u32[]{:S(2)}, u32[]{:S(2)}) collective-permute-start(s16[272,128]{1,0:T(8,128)(2,1)S(1)} %get-tuple-element.33), channel_id=1, source_target_pairs={{0,24},{4,28},{8,16},{12,20},{16,8},{20,12},{24,0},{28,4},{1,25},{... | collective-permute-start | bytes 208904 | tf_op jit(solution)/shard_map/ppermute | solution.py:326
  15.4 7.7 %collective-permute-start.3 = (s16[272,128]{1,0:T(8,128)(2,1)S(1)}, s16[272,128]{1,0:T(8,128)(2,1)S(1)}, u32[]{:S(2)}, u32[]{:S(2)}) collective-permute-start(s16[272,128]{1,0:T(8,128)(2,1)S(1)} %get-tuple-element.29), channel_id=1, source_target_pairs={{0,12},{4,8},{8,4},{12,0},{16,28},{20,24},{24,20},{28,16},{1,13},{... | collective-permute-start | bytes 208904 | tf_op jit(solution)/shard_map/ppermute | solution.py:339
  18.0 5.1 %collective-permute-start.4 = (s16[272,128]{1,0:T(8,128)(2,1)S(1)}, s16[272,128]{1,0:T(8,128)(2,1)S(1)}, u32[]{:S(2)}, u32[]{:S(2)}) collective-permute-start(s16[272,128]{1,0:T(8,128)(2,1)S(1)} %get-tuple-element.30), channel_id=1, source_target_pairs={{0,8},{4,12},{8,0},{12,4},{16,24},{20,28},{24,16},{28,20},{1,9},{5... | collective-permute-start | bytes 208904 | tf_op jit(solution)/shard_map/ppermute | solution.py:339
  18.5 4.6 %collective-permute-start.5 = (s16[272,128]{1,0:T(8,128)(2,1)S(1)}, s16[272,128]{1,0:T(8,128)(2,1)S(1)}, u32[]{:S(2)}, u32[]{:S(2)}) collective-permute-start(s16[272,128]{1,0:T(8,128)(2,1)S(1)} %get-tuple-element.31), channel_id=1, source_target_pairs={{0,4},{4,0},{8,12},{12,8},{16,20},{20,16},{24,28},{28,24},{1,5},{5... | collective-permute-start | bytes 208904 | tf_op jit(solution)/shard_map/ppermute | solution.py:339
  19.0 6.8 %collective-permute-start = (s16[272,128]{1,0:T(8,128)(2,1)S(1)}, s16[272,128]{1,0:T(8,128)(2,1)S(1)}, u32[]{:S(2)}, u32[]{:S(2)}) collective-permute-start(s16[272,128]{1,0:T(8,128)(2,1)S(1)} %get-tuple-element.23), channel_id=1, source_target_pairs={{0,16},{4,20},{8,24},{12,28},{16,0},{20,4},{24,8},{28,12},{1,17},{... | collective-permute-start | bytes 208904 | tf_op jit(solution)/shard_map/ppermute | solution.py:326

commit v7 on v6

--- a/solution.py
+++ b/solution.py
@@ -269,8 +269,9 @@
     scale = limit / jnp.maximum(jnp.sqrt(total), limit)
     rows = table_ref.shape[0]
     copies = []
-    for n in range(rows // step):
-        part = pl.ds(n * step, step)
+    cuts = [0, step // 4, *range(step, rows + 1, step)]
+    for n, (low, high) in enumerate(zip(cuts, cuts[1:])):
+        part = pl.ds(low, high - low)
         clipped = scale * grad_ref[part, :]
         new_first = beta_first * first_ref[part, :] + (1.0 - beta_first) * clipped
         first_buf[part, :] = new_first
@@ -381,7 +382,7 @@
         out_shape=(dense,) * 3,
         in_specs=[vmem] * 5,
         out_specs=(hbm,) * 3,
-        scratch_shapes=[pltpu.VMEM((rows_dev, width), f32)] * 3 + [pltpu.SemaphoreType.DMA((3, rows_dev // step))],
+        scratch_shapes=[pltpu.VMEM((rows_dev, width), f32)] * 3 + [pltpu.SemaphoreType.DMA((3, rows_dev // step + 1))],
         compiler_params=params(20),
         name="update_rows",
     )(parts, *[in_vmem(x) for x in (grad_rows, table_kept, first_kept, second_kept)])

time: 42.5 us -> 42.5 us (level)
  no operation moved by 1% of the time
where the time goes in v7:
time: 42.5 us; the launch traced here: 42.2 us
  Pallas kernels  16.5 us (39%)
  starting transfers between devices  14.5 us (34%)
  blocking collectives  10.4 us (24%)
  between operations  0.88 us (2%)
    ppermute x4, starting transfers between devices, body(): got[hop] = lax.ppermute(packed_far[hop - near], 'dp', hop_pairs(hop, peers))  10.9 us
    all_to_all x1, blocking collectives, body(): lax.all_to_all(part, ('dp', 'mp'), split_axis=0, concat_axis=0, tiled=True)  10.4 us
    pallas_call x1, Pallas kernels, body(): pl.pallas_call(functools.partial(update_kernel, limit, step), out_shape=(...  4.85 us
    pallas_call x3, Pallas kernels, body(): pl.pallas_call(functools.partial(join_kernel, group, room, opens, ends, m...  4.74 us
    pallas_call x1, Pallas kernels, body(): pl.pallas_call(functools.partial(pack_far_kernel, peers, rows_dev, room),...  4.6 us
    ppermute x3, starting transfers between devices, body(): got[hop] = lax.ppermute(packed_near[hop], 'dp', hop_pairs(hop, peers))  3.55 us
    pallas_call x1, Pallas kernels, body(): pl.pallas_call(functools.partial(pack_near_kernel, peers, rows_dev, room)...  2.26 us
  transfers between devices with their start and end apart: 7, of which 0 were waited for; matrix products, arithmetic and copies ran while one was open for 0% of the time, Pallas kernels for 14%

profile of v7, /device:TPU:0, one launch (start us, length us, event | category | flops | bytes accessed | tf_op | source)
XLA Modules:
  0.0 42.2 jit_solution(15045765575704654924)
XLA Ops:
  0.6 4.6 %pack_far.1 = (s16[272,128]{1,0:T(8,128)(2,1)S(1)}, s16[272,128]{1,0:T(8,128)(2,1)S(1)}, s16[272,128]{1,0:T(8,128)(2,1)S(1)}, s16[272,128]{1,0:T(8,128)(2,1)S(1)...) custom-call(s32[1,2048]{1,0:T(1,128)} %bitcast.1, ...), custom_call_target="tpu_custom_call" | custom-call | tf_op jit(solution)/shard_map/pack_far/pallas_call | solution.py:311
  5.2 6.0 %collective-permute-start.1 = (s16[272,128]{1,0:T(8,128)(2,1)S(1)}, s16[272,128]{1,0:T(8,128)(2,1)S(1)}, u32[]{:S(2)}, u32[]{:S(2)}) collective-permute-start(s16[272,128]{1,0:T(8,128)(2,1)S(1)} %get-tuple-element.24), channel_id=1, source_target_pairs={{0,28},{4,24},{8,20},{12,16},{16,12},{20,8},{24,4},{28,0},{1,29},{... | collective-permute-start | bytes 208904 | tf_op jit(solution)/shard_map/ppermute | solution.py:327
  11.3 0.0 collective-permute-start.2
  11.3 1.9 %collective-permute-start.6 = (s16[272,128]{1,0:T(8,128)(2,1)S(1)}, s16[272,128]{1,0:T(8,128)(2,1)S(1)}, u32[]{:S(2)}, u32[]{:S(2)}) collective-permute-start(s16[272,128]{1,0:T(8,128)(2,1)S(1)} %get-tuple-element.33), channel_id=1, source_target_pairs={{0,24},{4,28},{8,16},{12,20},{16,8},{20,12},{24,0},{28,4},{1,25},{... | collective-permute-start | bytes 208904 | tf_op jit(solution)/shard_map/ppermute | solution.py:327
  13.1 2.3 %pack_near.1 = (s16[272,128]{1,0:T(8,128)(2,1)S(1)}, s16[272,128]{1,0:T(8,128)(2,1)S(1)}, s16[272,128]{1,0:T(8,128)(2,1)S(1)}, s16[272,128]{1,0:T(8,128)(2,1)S(1)}, f32[8192,128]{1,0:T(8,128)S(1)}) custom-call(s32[1,2048]{1,0:T(1,128)S(1)} %get-tuple-element.26.rel_ref, s32[1,2048]{1,0:T(1,128)S(1)} %get-tuple-element.27.rank_ref, ...), custom_call_target="tpu_custom_call" | custom-call | flops 1073741824 | bytes 16777216 | tf_op jit(solution)/shard_map/pack_near/pallas_call | solution.py:328
  15.4 2.6 %collective-permute-start.3 = (s16[272,128]{1,0:T(8,128)(2,1)S(1)}, s16[272,128]{1,0:T(8,128)(2,1)S(1)}, u32[]{:S(2)}, u32[]{:S(2)}) collective-permute-start(s16[272,128]{1,0:T(8,128)(2,1)S(1)} %get-tuple-element.29), channel_id=1, source_target_pairs={{0,12},{4,8},{8,4},{12,0},{16,28},{20,24},{24,20},{28,16},{1,13},{... | collective-permute-start | bytes 208904 | tf_op jit(solution)/shard_map/ppermute | solution.py:340
  18.0 0.5 %collective-permute-start.4 = (s16[272,128]{1,0:T(8,128)(2,1)S(1)}, s16[272,128]{1,0:T(8,128)(2,1)S(1)}, u32[]{:S(2)}, u32[]{:S(2)}) collective-permute-start(s16[272,128]{1,0:T(8,128)(2,1)S(1)} %get-tuple-element.30), channel_id=1, source_target_pairs={{0,8},{4,12},{8,0},{12,4},{16,24},{20,28},{24,16},{28,20},{1,9},{5... | collective-permute-start | bytes 208904 | tf_op jit(solution)/shard_map/ppermute | solution.py:340
  18.5 0.0 collective-permute-done.1.refs_0_
  18.5 0.5 %collective-permute-start.5 = (s16[272,128]{1,0:T(8,128)(2,1)S(1)}, s16[272,128]{1,0:T(8,128)(2,1)S(1)}, u32[]{:S(2)}, u32[]{:S(2)}) collective-permute-start(s16[272,128]{1,0:T(8,128)(2,1)S(1)} %get-tuple-element.31), channel_id=1, source_target_pairs={{0,4},{4,0},{8,12},{12,8},{16,20},{20,16},{24,28},{28,24},{1,5},{5... | collective-permute-start | bytes 208904 | tf_op jit(solution)/shard_map/ppermute | solution.py:340
  19.0 0.0 collective-permute-done.6.refs_1_
  19.0 3.0 %collective-permute-start = (s16[272,128]{1,0:T(8,128)(2,1)S(1)}, s16[272,128]{1,0:T(8,128)(2,1)S(1)}, u32[]{:S(2)}, u32[]{:S(2)}) collective-permute-start(s16[272,128]{1,0:T(8,128)(2,1)S(1)} %get-tuple-element.23), channel_id=1, source_target_pairs={{0,16},{4,20},{8,24},{12,28},{16,0},{20,4},{24,8},{28,12},{1,17},{... | collective-permute-start | bytes 208904 | tf_op jit(solution)/shard_map/ppermute | solution.py:327
  22.0 1.1 %join_rows_0.1 = (f32[8200,128]{1,0:T(8,128)S(1)}, f32[8,128]{1,0:T(8,128)S(1)}) custom-call(s16[272,128]{1,0:T(8,128)(2,1)S(1)} %get-tuple-element.32.refs_0_, s16[272,128]{1,0:T(8,128)(2,1)S(1)} %collective-permute-done.6.refs_1_), custom_call_target="tpu_custom_call" | custom-call | flops 128 | bytes 128 | tf_op jit(solution)/shard_map/join_rows_0/pallas_call | solution.py:356
  23.1 0.0 collective-permute-done.2.refs_1_
  23.1 0.0 collective-permute-done.3.refs_2_
  23.1 0.0 collective-permute-done.4.refs_3_
  23.1 0.0 collective-permute-done.5.refs_4_
  23.1 2.7 %join_rows_1.1 = (f32[8200,128]{1,0:T(8,128)S(1)}, f32[8,128]{1,0:T(8,128)S(1)}, f32[8192,128]{1,0:T(8,128)S(1)}) custom-call(s16[272,128]{1,0:T(8,128)(2,1)S(1)} %collective-permute-done.1.refs_0_, s16[272,128]{1,0:T(8,128)(2,1)S(1)} %collective-permute-done.2.refs_1_, ...), custom_call_target="tpu_custom_call", output_to_operand_aliasing={{0}: (5, {})} | custom-call | flops 128 | bytes 128 | tf_op jit(solution)/shard_map/join_rows_1/pallas_call | solution.py:356
  25.8 0.0 collective-permute-done.refs_0_
  25.8 1.0 %join_rows_2.1 = (f32[8200,128]{1,0:T(8,128)S(1)}, f32[32,1,128]{2,1,0:T(1,128)S(1)}) custom-call(s16[272,128]{1,0:T(8,128)(2,1)S(1)} %collective-permute-done.refs_0_, f32[8200,128]{1,0:T(8,128)S(1)} %get-tuple-element.36.refs_1_, f32[8,128]{1,0:T(8,128)S(1)} %get-tuple-element.37.refs_2_), custom_call_target="tpu_custom_call", output_to_operand_aliasing={{0}: (1, {})} | custom-call | flops 128 | bytes 128 | tf_op jit(solution)/shard_map/join_rows_2/pallas_call | solution.py:356
  26.8 10.4 %all_to_all.5.parts_ref = f32[32,1,128]{2,1,0:T(1,128)S(1)} all-to-all(f32[32,1,128]{2,1,0:T(1,128)S(1)} %get-tuple-element.38), channel_id=1, replica_groups=mesh['dp'=8,'mp'=4] {'dp','mp'}, dimensions={0} | all-to-all | bytes 32768 | tf_op jit(solution)/shard_map/all_to_all | solution.py:377
  37.2 4.8 %update_rows.1 = (f32[8192,128]{1,0:T(8,128)}, f32[8192,128]{1,0:T(8,128)}, f32[8192,128]{1,0:T(8,128)}) custom-call(f32[32,1,128]{2,1,0:T(1,128)S(1)} %all_to_all.5.parts_ref, f32[8200,128]{1,0:T(8,128)S(1)} %get-tuple-element.39.grad_ref, f32[8192,128]{1,0:T(8,128)S(1)} %get-tuple-element.40.table_ref, f32[8192,128]{1,0:T(8,128)S(1)} %get-tuple-element.41.first_ref, ...), custom_call_target="tpu_custom_call" | custom-call | tf_op jit(solution)/shard_map/update_rows/pallas_call | solution.py:380
Async XLA Ops:
  5.2 13.2 %collective-permute-start.1 = (s16[272,128]{1,0:T(8,128)(2,1)S(1)}, s16[272,128]{1,0:T(8,128)(2,1)S(1)}, u32[]{:S(2)}, u32[]{:S(2)}) collective-permute-start(s16[272,128]{1,0:T(8,128)(2,1)S(1)} %get-tuple-element.24), channel_id=1, source_target_pairs={{0,28},{4,24},{8,20},{12,16},{16,12},{20,8},{24,4},{28,0},{1,29},{... | collective-permute-start | bytes 208904 | tf_op jit(solution)/shard_map/ppermute | solution.py:327
  11.3 11.8 %collective-permute-start.2 = (s16[272,128]{1,0:T(8,128)(2,1)S(1)}, s16[272,128]{1,0:T(8,128)(2,1)S(1)}, u32[]{:S(2)}, u32[]{:S(2)}) collective-permute-start(s16[272,128]{1,0:T(8,128)(2,1)S(1)} %get-tuple-element.25), channel_id=1, source_target_pairs={{0,20},{4,16},{8,28},{12,24},{16,4},{20,0},{24,12},{28,8},{1,21},{... | collective-permute-start | bytes 208904 | tf_op jit(solution)/shard_map/ppermute | solution.py:327
  11.3 7.7 %collective-permute-start.6 = (s16[272,128]{1,0:T(8,128)(2,1)S(1)}, s16[272,128]{1,0:T(8,128)(2,1)S(1)}, u32[]{:S(2)}, u32[]{:S(2)}) collective-permute-start(s16[272,128]{1,0:T(8,128)(2,1)S(1)} %get-tuple-element.33), channel_id=1, source_target_pairs={{0,24},{4,28},{8,16},{12,20},{16,8},{20,12},{24,0},{28,4},{1,25},{... | collective-permute-start | bytes 208904 | tf_op jit(solution)/shard_map/ppermute | solution.py:327
  15.4 7.7 %collective-permute-start.3 = (s16[272,128]{1,0:T(8,128)(2,1)S(1)}, s16[272,128]{1,0:T(8,128)(2,1)S(1)}, u32[]{:S(2)}, u32[]{:S(2)}) collective-permute-start(s16[272,128]{1,0:T(8,128)(2,1)S(1)} %get-tuple-element.29), channel_id=1, source_target_pairs={{0,12},{4,8},{8,4},{12,0},{16,28},{20,24},{24,20},{28,16},{1,13},{... | collective-permute-start | bytes 208904 | tf_op jit(solution)/shard_map/ppermute | solution.py:340
  18.0 5.1 %collective-permute-start.4 = (s16[272,128]{1,0:T(8,128)(2,1)S(1)}, s16[272,128]{1,0:T(8,128)(2,1)S(1)}, u32[]{:S(2)}, u32[]{:S(2)}) collective-permute-start(s16[272,128]{1,0:T(8,128)(2,1)S(1)} %get-tuple-element.30), channel_id=1, source_target_pairs={{0,8},{4,12},{8,0},{12,4},{16,24},{20,28},{24,16},{28,20},{1,9},{5... | collective-permute-start | bytes 208904 | tf_op jit(solution)/shard_map/ppermute | solution.py:340
  18.5 4.6 %collective-permute-start.5 = (s16[272,128]{1,0:T(8,128)(2,1)S(1)}, s16[272,128]{1,0:T(8,128)(2,1)S(1)}, u32[]{:S(2)}, u32[]{:S(2)}) collective-permute-start(s16[272,128]{1,0:T(8,128)(2,1)S(1)} %get-tuple-element.31), channel_id=1, source_target_pairs={{0,4},{4,0},{8,12},{12,8},{16,20},{20,16},{24,28},{28,24},{1,5},{5... | collective-permute-start | bytes 208904 | tf_op jit(solution)/shard_map/ppermute | solution.py:340
  19.0 6.8 %collective-permute-start = (s16[272,128]{1,0:T(8,128)(2,1)S(1)}, s16[272,128]{1,0:T(8,128)(2,1)S(1)}, u32[]{:S(2)}, u32[]{:S(2)}) collective-permute-start(s16[272,128]{1,0:T(8,128)(2,1)S(1)} %get-tuple-element.23), channel_id=1, source_target_pairs={{0,16},{4,20},{8,24},{12,28},{16,0},{20,4},{24,8},{28,12},{1,17},{... | collective-permute-start | bytes 208904 | tf_op jit(solution)/shard_map/ppermute | solution.py:327
